TPU v7x, 256 devices: a whole 4x4x8 slice. The times are simulated.
256 devices in a mesh: dp: 4 (over y), ctx: 16 (over x, z_lo), tp: 4 (over z_hi, core).
Axes of the slice: x: 4, y: 4, z: 8 (z_hi: 2, z_lo: 4; z = z_hi * 4 + z_lo), core: 2. Of those that a mesh axis runs over, the one named last changes fastest.
Arguments:
- normed: bfloat16 [4, 2048, 4096], P('dp', 'ctx'), may hold values from -24 to 24
- w_qkv: bfloat16 [4096, 3072], P(('dp', 'ctx'), 'tp'), may hold values from -0.09765625 to 0.09765625
- w_out: bfloat16 [4096, 2048], P(('dp', 'ctx'), 'tp'), may hold values from -0.125 to 0.125
- block_order: int32 [32], replicated, may hold values from 0 to 31, each once
- d_out: bfloat16 [4, 2048, 4096], P('dp', 'ctx'), may hold values from -6 to 6
Outputs:
- attn_out: bfloat16 [4, 2048, 4096], P('dp', 'ctx', 'tp')
- d_normed: bfloat16 [4, 2048, 4096], P('dp', 'ctx', 'tp')
- d_w_qkv: bfloat16 [4096, 3072], P(('dp', 'ctx'), 'tp')
- d_w_out: bfloat16 [4096, 2048], P(('dp', 'ctx'), 'tp')
Inputs may be any that keep to these rules, and one draw needn't show every extreme that they name: `block_order`: each number appears once.
All inputs are finite; a program needn't handle non-finite values.
Results may differ from a plain program's by a relative error of at most 0.035.
Values may be sent and summed in bfloat16 or wider, within the bound.
A program may use at most 128 MiB of HBM per device.

v0:
```python
import jax
import jax.numpy as jnp
from jax import lax
from jax.sharding import PartitionSpec as P

HD = 128


rope_base = 500000.0
masked_score = -1e30


def stored_positions(order, row_ids, block_rows):
    owner = row_ids // block_rows
    matches = owner[:, None] == jnp.arange(order.shape[0], dtype=jnp.int32)[None, :]
    picked = jnp.sum(jnp.where(matches, order[None, :], 0), axis=1)
    return picked * block_rows + row_ids % block_rows


def rope_tables(positions, head_size):
    half_size = head_size // 2
    frequency = rope_base ** (-2.0 * jnp.arange(half_size, dtype=jnp.float32) / head_size)
    angles = positions.astype(jnp.float32)[:, None] * frequency[None, :]
    angles = jnp.concatenate([angles, angles], axis=1)
    return (jnp.cos(angles), jnp.sin(angles))


def rotate_half(values):
    half_size = values.shape[-1] // 2
    return jnp.concatenate([-values[..., half_size:], values[..., :half_size]], axis=-1)


def apply_rope(values, cosine, sines, direction_sign):
    table_shape = (cosine.shape[0],) + (1,) * (values.ndim - 2) + (cosine.shape[1],)
    return values * cosine.reshape(table_shape) + direction_sign * rotate_half(
        values
    ) * sines.reshape(table_shape)


def round_bfloat(values):
    return lax.optimization_barrier(values.astype(jnp.bfloat16)).astype(jnp.float32)


def attend_keys(state, key_rows, value_rows, key_pos, queries, query_pos, score_scale):
    row_max, row_sum, weighted = state
    scores = (
        jnp.einsum("tkgd,skd->kgts", queries, key_rows, preferred_element_type=jnp.float32)
        * score_scale
    )
    allowed = key_pos[None, :] <= query_pos[:, None]
    scores = jnp.where(allowed, scores, masked_score)
    new_max = jnp.maximum(row_max, jnp.max(scores, axis=-1))
    raw = jnp.where(allowed, jnp.exp(scores - new_max[..., None]), 0.0)
    factor = jnp.exp(row_max - new_max)
    row_sum = row_sum * factor + jnp.sum(raw, axis=-1)
    weighted = weighted * factor[..., None] + jnp.einsum(
        "kgts,skd->kgtd", raw.astype(jnp.bfloat16), value_rows, preferred_element_type=jnp.float32
    )
    return ((new_max, row_sum, weighted), scores)


def maybe_attend(state, key_rows, value_rows, key_pos, queries, query_pos, score_scale):
    return attend_keys(state, key_rows, value_rows, key_pos, queries, query_pos, score_scale)


def block_grads(
    dq_sum,
    key_rows,
    value_rows,
    key_pos,
    block_scores,
    queries,
    query_pos,
    grads_four,
    row_dots,
    row_max,
    row_sum,
    score_scale,
):
    allowed = key_pos[None, :] <= query_pos[:, None]
    weights = jnp.where(
        allowed, jnp.exp(block_scores - row_max[..., None]) / row_sum[..., None], 0.0
    )
    dweights = jnp.einsum(
        "tkgd,skd->kgts", grads_four, value_rows, preferred_element_type=jnp.float32
    )
    dscores = (weights * (dweights - row_dots[..., None])).astype(jnp.bfloat16)
    dq_sum = dq_sum + jnp.einsum(
        "kgts,skd->tkgd", dscores, key_rows, preferred_element_type=jnp.float32
    )
    key_grad = (
        jnp.einsum("kgts,tkgd->skd", dscores, queries, preferred_element_type=jnp.float32)
        * score_scale
    )
    value_grad = jnp.einsum(
        "kgts,tkgd->skd",
        weights.astype(jnp.bfloat16),
        grads_four,
        preferred_element_type=jnp.float32,
    )
    return (dq_sum, key_grad, value_grad)


def body(normed, w_qkv, w_out, block_order, d_out):
    local_rows = normed.shape[1]
    block_rows = local_rows // 2
    head_size = HD
    q_width = w_out.shape[1]
    kv_width = (w_qkv.shape[1] - q_width) // 2
    head_count = q_width // head_size
    kv_count = kv_width // head_size
    group_size = head_count // kv_count
    score_scale = head_size ** (-0.5)
    ctx_count = lax.axis_size("ctx")
    length = local_rows * ctx_count
    ctx_index = lax.axis_index("ctx")
    query_pos = stored_positions(
        block_order, ctx_index * local_rows + jnp.arange(local_rows, dtype=jnp.int32), block_rows
    )
    all_pos = stored_positions(block_order, jnp.arange(length, dtype=jnp.int32), block_rows)
    widen = 1
    while widen * 2 <= ctx_count and ctx_count % (widen * 2) == 0 and (local_rows * widen < 512):
        widen = widen * 2
    key_span = local_rows * widen
    key_blocks = length // key_span
    qkv_weight, out_weight = (
        lax.all_gather(w_qkv, ("dp", "ctx"), axis=0, tiled=True),
        lax.all_gather(w_out, ("dp", "ctx"), axis=0, tiled=True),
    )
    tokens = normed[0]
    projected = jnp.dot(tokens, qkv_weight, preferred_element_type=jnp.float32)
    cosine, sines = rope_tables(query_pos, head_size)
    queries = apply_rope(
        projected[:, :q_width].reshape(local_rows, kv_count, group_size, head_size),
        cosine,
        sines,
        1.0,
    ).astype(jnp.bfloat16)
    key_rows = apply_rope(
        projected[:, q_width : q_width + kv_width].reshape(local_rows, kv_count, head_size),
        cosine,
        sines,
        1.0,
    ).astype(jnp.bfloat16)
    value_rows = (
        projected[:, q_width + kv_width :]
        .reshape(local_rows, kv_count, head_size)
        .astype(jnp.bfloat16)
    )
    start_state = (
        jnp.full((kv_count, group_size, local_rows), masked_score, jnp.float32),
        jnp.zeros((kv_count, group_size, local_rows), jnp.float32),
        jnp.zeros((kv_count, group_size, local_rows, head_size), jnp.float32),
    )
    all_keys, all_values = (
        lax.all_gather(key_rows, "ctx", axis=0, tiled=True),
        lax.all_gather(value_rows, "ctx", axis=0, tiled=True),
    )

    def local_step(state, pieces):
        return maybe_attend(state, pieces[0], pieces[1], pieces[2], queries, query_pos, score_scale)

    final_state, score_blocks = lax.scan(
        local_step,
        start_state,
        (
            all_keys.reshape(key_blocks, key_span, kv_count, head_size),
            all_values.reshape(key_blocks, key_span, kv_count, head_size),
            all_pos.reshape(key_blocks, key_span),
        ),
    )
    row_max, row_sum, weighted = final_state
    attended = weighted / row_sum[..., None]
    heads_out = (
        jnp.transpose(attended, (2, 0, 1, 3)).reshape(local_rows, q_width).astype(jnp.bfloat16)
    )
    out_term = round_bfloat(
        jnp.einsum("th,dh->td", heads_out, out_weight, preferred_element_type=jnp.float32)
    )
    upstream = d_out[0]
    head_grads = jnp.dot(upstream, out_weight, preferred_element_type=jnp.float32).astype(
        jnp.bfloat16
    )
    out_weight_term = round_bfloat(
        jnp.einsum("td,th->dh", upstream, heads_out, preferred_element_type=jnp.float32)
    )
    grads_four = head_grads.reshape(local_rows, kv_count, group_size, head_size)
    out_four = heads_out.reshape(local_rows, kv_count, group_size, head_size)
    row_dots = jnp.einsum(
        "tkgd,tkgd->kgt", grads_four.astype(jnp.float32), out_four.astype(jnp.float32)
    )

    def back_step(dq_sum, pieces):
        block_keys, block_values, block_pos, block_scores = pieces
        dq_sum, key_grad, value_grad = block_grads(
            dq_sum,
            block_keys,
            block_values,
            block_pos,
            block_scores,
            queries,
            query_pos,
            grads_four,
            row_dots,
            row_max,
            row_sum,
            score_scale,
        )
        return (dq_sum, (key_grad, value_grad))

    dq_start = jnp.zeros((local_rows, kv_count, group_size, head_size), jnp.float32)
    dq_sum, block_outputs = lax.scan(
        back_step,
        dq_start,
        (
            all_keys.reshape(key_blocks, key_span, kv_count, head_size),
            all_values.reshape(key_blocks, key_span, kv_count, head_size),
            all_pos.reshape(key_blocks, key_span),
            score_blocks,
        ),
    )
    key_grad_all = block_outputs[0].reshape(length, kv_count, head_size)
    value_grad_all = block_outputs[1].reshape(length, kv_count, head_size)
    key_grad, value_grad = (
        lax.psum_scatter(
            key_grad_all.astype(jnp.bfloat16), "ctx", scatter_dimension=0, tiled=True
        ).astype(jnp.float32),
        lax.psum_scatter(
            value_grad_all.astype(jnp.bfloat16), "ctx", scatter_dimension=0, tiled=True
        ).astype(jnp.float32),
    )
    query_pre = apply_rope(dq_sum * score_scale, cosine, sines, -1.0)
    key_pre = apply_rope(key_grad, cosine, sines, -1.0)
    qkv_grads = jnp.concatenate(
        [
            query_pre.reshape(local_rows, q_width),
            key_pre.reshape(local_rows, kv_width),
            value_grad.reshape(local_rows, kv_width),
        ],
        axis=1,
    ).astype(jnp.bfloat16)
    input_term = round_bfloat(
        jnp.einsum("tc,dc->td", qkv_grads, qkv_weight, preferred_element_type=jnp.float32)
    )
    qkv_weight_term = round_bfloat(
        jnp.einsum("td,tc->dc", tokens, qkv_grads, preferred_element_type=jnp.float32)
    )
    out_share, input_share = (
        lax.psum_scatter(
            out_term.astype(jnp.bfloat16), "tp", scatter_dimension=1, tiled=True
        ).astype(jnp.float32),
        lax.psum_scatter(
            input_term.astype(jnp.bfloat16), "tp", scatter_dimension=1, tiled=True
        ).astype(jnp.float32),
    )
    dp_sums = (
        lax.psum_scatter(
            qkv_weight_term.astype(jnp.bfloat16), "dp", scatter_dimension=0, tiled=True
        ).astype(jnp.float32),
        lax.psum_scatter(
            out_weight_term.astype(jnp.bfloat16), "dp", scatter_dimension=0, tiled=True
        ).astype(jnp.float32),
    )
    qkv_rounded = round_bfloat(dp_sums[0])
    out_rounded = round_bfloat(dp_sums[1])
    ctx_sums = (
        lax.psum_scatter(
            qkv_rounded.astype(jnp.bfloat16), "ctx", scatter_dimension=0, tiled=True
        ).astype(jnp.float32),
        lax.psum_scatter(
            out_rounded.astype(jnp.bfloat16), "ctx", scatter_dimension=0, tiled=True
        ).astype(jnp.float32),
    )
    return (
        out_share.astype(jnp.bfloat16)[None],
        input_share.astype(jnp.bfloat16)[None],
        ctx_sums[0].astype(jnp.bfloat16),
        ctx_sums[1].astype(jnp.bfloat16),
    )


def solution(mesh):
    in_specs = (
        P("dp", "ctx", None),
        P(("dp", "ctx"), "tp"),
        P(("dp", "ctx"), "tp"),
        P(),
        P("dp", "ctx", None),
    )
    out_specs = (
        P("dp", "ctx", "tp"),
        P("dp", "ctx", "tp"),
        P(("dp", "ctx"), "tp"),
        P(("dp", "ctx"), "tp"),
    )
    return jax.shard_map(body, mesh=mesh, in_specs=in_specs, out_specs=out_specs, check_vma=False)
```

profile of v0, /device:TPU:64, one launch (start us, length us, event | category | flops | bytes accessed | tf_op | source)
XLA Modules:
  0.0 1429.8 jit_solution(7684336262470580907)
XLA Ops:
  11.1 358.5 %all-gather.7.cloned.1.call-done = bf16[4096,512]{1,0:T(8,128)(2,1)} async-done(((bf16[64,512]{1,0:T(8,128)(2,1)}), bf16[4096,512]{1,0:T(8,128)(2,1)}) %all-gather.7.cloned.1.call-update) | async-done | bytes 4194320 | tf_op jit(solution)/shard_map/all_gather | solution.py:128
  369.6 3.2 convolution_convert_fusion.4
  374.5 362.8 %all-gather.5.cloned.1.call-done = bf16[4096,768]{1,0:T(8,128)(2,1)} async-done(((bf16[64,768]{1,0:T(8,128)(2,1)}), bf16[4096,768]{1,0:T(8,128)(2,1)}) %all-gather.5.cloned.1.call-update) | async-done | bytes 6291472 | tf_op jit(solution)/shard_map/all_gather | solution.py:127
  737.2 3.8 fusion.56
  741.8 39.7 %all-gather = bf16[2048,128]{1,0:T(8,128)(2,1)S(1)} all-gather(bf16[128,128]{1,0:T(8,128)(2,1)S(1)} %get-tuple-element.392), channel_id=2, replica_groups=mesh['dp'=4,'ctx'=16,'tp'=4] {'ctx'}, dimensions={0}, use_global_device_ids=true | all-gather | bytes 557056 | tf_op jit(solution)/shard_map/all_gather | solution.py:156
  781.4 43.9 %all-gather.1 = bf16[2048,128]{1,0:T(8,128)(2,1)} all-gather(bf16[128,128]{1,0:T(8,128)(2,1)S(1)} %slice.66), channel_id=3, replica_groups=mesh['dp'=4,'ctx'=16,'tp'=4] {'ctx'}, dimensions={0}, use_global_device_ids=true | all-gather | bytes 557056 | tf_op jit(solution)/shard_map/all_gather | solution.py:157
  825.5 19.7 %while.32 = (s32[]{:T(128)}, f32[1,4,128]{2,1,0:T(4,128)S(1)}, f32[1,4,128]{2,1,0:T(4,128)}, f32[1,4,128,128]{3,2,1,0:T(8,128)S(1)}, f32[4,1,4,128,512]{3,4,2,1,...) while((s32[]{:T(128)}, f32[1,4,128]{2,1,0:T(4,128)S(1)}, ...), condition=%wide.region_5.6_spmd.clone, body=%wide.region_2.5_spmd.clone.sunk | while | flops 136842240 | bytes 6463113 | solution.py:163
  826.6 1.3 fusion.114
  828.8 1.1 bitcast_dynamic-update-slice_fusion.2
  831.0 1.3 fusion.114
  832.6 1.3 bitcast_add_fusion.2
  833.9 1.1 bitcast_dynamic-update-slice_fusion.2
  836.1 1.3 fusion.114
  837.7 1.3 bitcast_add_fusion.2
  839.0 1.1 bitcast_dynamic-update-slice_fusion.2
  841.2 1.3 fusion.114
  842.8 1.3 bitcast_add_fusion.2
  844.1 1.0 bitcast_dynamic-update-slice_fusion.2
  845.3 1.0 multiply_reduce_fusion
  846.3 23.1 %while.33 = (s32[]{:T(128)}, f32[128,1,4,128]{0,3,2,1:T(8,128)S(1)}, bf16[4,512,1,128]{3,1,2,0:T(8,128)(2,1)}, bf16[4,512,1,128]{3,1,2,0:T(8,128)(2,1)}, bf16[4,...) while((s32[]{:T(128)}, ...), condition=%wide.region_8.9_spmd.clone, body=%wide.region_7.8_spmd.clone.sunk | while | flops 271319040 | bytes 9792255 | solution.py:212
  846.3 0.9 broadcast_compare_fusion.5
  847.2 1.8 fusion.123
  849.7 2.4 fusion.126
  852.1 0.9 broadcast_compare_fusion.5
  853.0 1.8 fusion.123
  855.4 2.4 fusion.126
  857.9 0.9 broadcast_compare_fusion.5
  858.7 1.8 fusion.123
  861.2 2.4 fusion.126
  863.6 0.9 broadcast_compare_fusion.5
  864.5 1.8 fusion.123
  867.0 2.4 fusion.126
  870.0 4.4 fusion.52
  874.8 79.9 %reduce-scatter.15.cloned.1.call-done = bf16[128,1,128]{2,0,1:T(8,128)(2,1)} async-done(((bf16[2048,1,128]{2,0,1:T(8,128)(2,1)}), bf16[128,1,128]{2,0,1:T(8,128)(2,1)}) %reduce-scatter.15.cloned.1.call-update) | async-done | bytes 32784 | tf_op jit(solution)/shard_map/reduce_scatter | solution.py:225
  956.3 1.1 fusion.70
  957.5 80.7 %reduce-scatter.17.cloned.1.call-done = bf16[128,1,128]{2,0,1:T(8,128)(2,1)} async-done(((bf16[2048,1,128]{2,0,1:T(8,128)(2,1)}), bf16[128,1,128]{2,0,1:T(8,128)(2,1)}) %reduce-scatter.17.cloned.1.call-update) | async-done | bytes 32784 | tf_op jit(solution)/shard_map/reduce_scatter | solution.py:228
  1038.2 0.9 copy.73
  1039.1 4.4 fusion.51
  1043.6 4.7 convolution_convert_fusion.3
  1048.3 6.0 convolution_convert_fusion.2
  1054.4 37.0 %reduce-scatter.23.cloned.1.call-done = bf16[1024,512]{0,1:T(8,128)(2,1)} async-done(((bf16[4096,512]{0,1:T(8,128)(2,1)}), bf16[1024,512]{0,1:T(8,128)(2,1)}) %reduce-scatter.23.cloned.1.call-update) | async-done | bytes 1048592 | tf_op jit(solution)/shard_map/reduce_scatter | solution.py:260
  1091.5 2.3 copy.86
  1093.8 66.4 %reduce-scatter.21.cloned.1.call-done = bf16[1024,768]{0,1:T(8,128)(2,1)} async-done(((bf16[4096,768]{0,1:T(8,128)(2,1)}), bf16[1024,768]{0,1:T(8,128)(2,1)}) %reduce-scatter.21.cloned.1.call-update) | async-done | bytes 1572880 | tf_op jit(solution)/shard_map/reduce_scatter | solution.py:257
  1160.3 2.6 copy.84
  1162.9 43.8 %reduce-scatter.13.cloned.1.call-done = bf16[128,1024]{1,0:T(8,128)(2,1)} async-done(((bf16[128,4096]{1,0:T(8,128)(2,1)}), bf16[128,1024]{1,0:T(8,128)(2,1)}) %reduce-scatter.13.cloned.1.call-update) | async-done | bytes 262160 | tf_op jit(solution)/shard_map/reduce_scatter | solution.py:249
  1206.7 44.9 %reduce-scatter.19.cloned.1.call-done = bf16[128,1024]{1,0:T(8,128)(2,1)} async-done(((bf16[128,4096]{1,0:T(8,128)(2,1)}), bf16[128,1024]{1,0:T(8,128)(2,1)}) %reduce-scatter.19.cloned.1.call-update) | async-done | bytes 262160 | tf_op jit(solution)/shard_map/reduce_scatter | solution.py:252
  1251.6 83.6 %reduce-scatter.27.cloned.1.call-done = bf16[64,512]{1,0:T(8,128)(2,1)} async-done(((bf16[1024,512]{1,0:T(8,128)(2,1)}), bf16[64,512]{1,0:T(8,128)(2,1)}) %reduce-scatter.27.cloned.1.call-update) | async-done | bytes 65552
  1335.1 87.9 %reduce-scatter.25.cloned.1.call-done = bf16[64,768]{1,0:T(8,128)(2,1)} async-done(((bf16[1024,768]{1,0:T(8,128)(2,1)}), bf16[64,768]{1,0:T(8,128)(2,1)}) %reduce-scatter.25.cloned.1.call-update) | async-done | bytes 98320
  (124 shorter events, 17.8 us)
Async XLA Ops:
  7.2 730.1 %copy-start = (bf16[1,128,4096]{2,1,0:T(8,128)(2,1)S(1)}, bf16[1,128,4096]{2,1,0:T(8,128)(2,1)}, u32[]{:S(2)}) copy-start(bf16[1,128,4096]{2,1,0:T(8,128)(2,1)} %param.9) | copy-start | bytes 3145732
  7.2 362.4 %all-gather.7.cloned.1.call-start = ((), (), s32[]{:S(2)}) async-start(), calls=%async_computation.9 | async-start | bytes 4259840 | tf_op jit(solution)/shard_map/all_gather | solution.py:128
  7.9 729.3 %all-gather.5.cloned.1.call-start = ((), (), s32[]{:S(2)}) async-start(), calls=%async_computation.8 | async-start | bytes 6389760 | tf_op jit(solution)/shard_map/all_gather | solution.py:127
  8.7 946.0 %reduce-scatter.15.cloned.1.call-start = ((), (), s32[]{:S(2)}) async-start(), calls=%async_computation.11 | async-start | bytes 557056 | tf_op jit(solution)/shard_map/reduce_scatter | solution.py:225
  846.3 3.0 copy-start.1
  846.3 3.4 copy-start.3
  849.6 2.4 copy-start.2
  852.1 3.0 copy-start.1
  852.1 3.3 copy-start.3
  855.4 2.4 copy-start.2
  857.8 3.0 copy-start.1
  857.8 3.3 copy-start.3
  861.2 2.4 copy-start.2
  863.6 3.0 copy-start.1
  863.6 3.3 copy-start.3
  866.9 2.4 copy-start.2
  869.4 168.9 %reduce-scatter.17.cloned.1.call-start = ((), (), s32[]{:S(2)}) async-start(), calls=%async_computation.12 | async-start | bytes 557056 | tf_op jit(solution)/shard_map/reduce_scatter | solution.py:228
  870.0 221.5 %reduce-scatter.23.cloned.1.call-start = ((), (), s32[]{:S(2)}) async-start(), calls=%async_computation.15 | async-start | bytes 5242880 | tf_op jit(solution)/shard_map/reduce_scatter | solution.py:260
  874.4 285.8 %reduce-scatter.21.cloned.1.call-start = ((), (), s32[]{:S(2)}) async-start(), calls=%async_computation.14 | async-start | bytes 7864320 | tf_op jit(solution)/shard_map/reduce_scatter | solution.py:257
  1043.6 163.1 %reduce-scatter.13.cloned.1.call-start = ((), (), s32[]{:S(2)}) async-start(), calls=%async_computation.10 | async-start | bytes 1310720 | tf_op jit(solution)/shard_map/reduce_scatter | solution.py:249
  1048.3 203.3 %reduce-scatter.19.cloned.1.call-start = ((), (), s32[]{:S(2)}) async-start(), calls=%async_computation.13 | async-start | bytes 1310720 | tf_op jit(solution)/shard_map/reduce_scatter | solution.py:252
  1054.4 280.8 %reduce-scatter.27.cloned.1.call-start = ((), (), s32[]{:S(2)}) async-start(), calls=%async_computation.17 | async-start | bytes 1114112
  1093.8 329.2 %reduce-scatter.25.cloned.1.call-start = ((), (), s32[]{:S(2)}) async-start(), calls=%async_computation.16 | async-start | bytes 1671168
Sparse Core Ops, SparseCore 0:
  9.8 359.7 all-gather.6
  371.4 365.8 all-gather.4
  869.5 85.1 reduce-scatter.14
  957.2 81.0 reduce-scatter.16
  1040.6 50.7 reduce-scatter.22
  1094.0 66.1 reduce-scatter.20
  1163.8 42.7 reduce-scatter.12
  1210.0 41.5 reduce-scatter.18
  1254.8 80.2 reduce-scatter.26
  1338.1 84.8 reduce-scatter.24
where the time goes:
time: 1440 us; the launch traced here: 1430 us
  waiting for transfers between devices  1250 us (87%)
  blocking collectives  83.6 us (6%)
  matrix products  52.4 us (4%)
  other arithmetic  17.9 us (1%)
  between operations  14.5 us (1%)
    all_gather x1, waiting for transfers between devices, body(): lax.all_gather(w_qkv, ('dp', 'ctx'), axis=0, tiled=True)  363 us
    all_gather x1, waiting for transfers between devices, body(): lax.all_gather(w_out, ('dp', 'ctx'), axis=0, tiled=True)  359 us
    unnamed x12, waiting for transfers between devices  173 us
    reduce_scatter x1, waiting for transfers between devices, body(): lax.psum_scatter(value_grad_all.astype(jnp.bfloat16), 'ctx', scatter_dime...  80.7 us
    reduce_scatter x1, waiting for transfers between devices, body(): lax.psum_scatter(key_grad_all.astype(jnp.bfloat16), 'ctx', scatter_dimens...  79.9 us
    reduce_scatter x1, waiting for transfers between devices, body(): lax.psum_scatter(qkv_weight_term.astype(jnp.bfloat16), 'dp', scatter_dime...  66.4 us
    reduce_scatter x1, waiting for transfers between devices, body(): lax.psum_scatter(input_term.astype(jnp.bfloat16), 'tp', scatter_dimension...  44.9 us
    all_gather x1, blocking collectives, body(): lax.all_gather(value_rows, 'ctx', axis=0, tiled=True)  43.9 us
  transfers between devices with their start and end apart: 10, of which 10 were waited for; matrix products, arithmetic and copies ran while one was open for 2% of the time, Pallas kernels for 0%

commit v1 on v0

v1 whole, which is shorter than its diff:
```python
import jax
import jax.numpy as jnp
from jax import lax
from jax.experimental import pallas as pl
from jax.experimental.pallas import tpu as pltpu
from jax.sharding import PartitionSpec as P

HD = 128
SIDE = 4
MESH = pl.DeviceIdType.MESH

rope_base = 500000.0
masked_score = -1e30


def stored_positions(order, row_ids, block_rows):
    owner = row_ids // block_rows
    matches = owner[:, None] == jnp.arange(order.shape[0], dtype=jnp.int32)[None, :]
    picked = jnp.sum(jnp.where(matches, order[None, :], 0), axis=1)
    return picked * block_rows + row_ids % block_rows


def rope_tables(positions, head_size):
    half_size = head_size // 2
    frequency = rope_base ** (-2.0 * jnp.arange(half_size, dtype=jnp.float32) / head_size)
    angles = positions.astype(jnp.float32)[:, None] * frequency[None, :]
    angles = jnp.concatenate([angles, angles], axis=1)
    return (jnp.cos(angles), jnp.sin(angles))


def rotate_half(values):
    half_size = values.shape[-1] // 2
    return jnp.concatenate([-values[..., half_size:], values[..., :half_size]], axis=-1)


def apply_rope(values, cosine, sines, direction_sign):
    return values * cosine[:, None, :] + direction_sign * rotate_half(values) * sines[:, None, :]


class Links:
    def __init__(self, send, recv):
        self.send, self.recv, self.used, self.copies = send, recv, 0, []
        self.y = lax.axis_index("dp")
        self.c = lax.axis_index("ctx")
        self.t = lax.axis_index("tp")
        self.x = self.c // SIDE
        self.z = self.c % SIDE

    def along_y(self, k):
        return (lax.rem(self.y + k, SIDE), self.c, self.t)

    def along_x(self, k):
        return (self.y, lax.rem(self.x + k, SIDE) * SIDE + self.z, self.t)

    def along_z(self, k):
        return (self.y, self.x * SIDE + lax.rem(self.z + k, SIDE), self.t)

    def other_core(self):
        return (self.y, self.c, self.t + 1 - 2 * lax.rem(self.t, 2))

    def other_side(self):
        return (self.y, self.c, lax.rem(self.t + 2, 4))

    def greet(self, partners):
        barrier = pltpu.get_barrier_semaphore()
        for partner in partners:
            pl.semaphore_signal(barrier, inc=1, device_id=partner, device_id_type=MESH)
        pl.semaphore_wait(barrier, len(partners))

    def copy(self, source, target, partner):
        made = pltpu.make_async_remote_copy(
            src_ref=source,
            dst_ref=target,
            send_sem=self.send.at[self.used],
            recv_sem=self.recv.at[self.used],
            device_id=partner,
            device_id_type=MESH,
        )
        made.start()
        self.used += 1
        self.copies.append(made)
        return made

    def finish(self):
        for made in self.copies:
            made.wait_send()


def interleave(streams):
    streams = list(streams)
    while streams:
        left = []
        for stream in streams:
            try:
                next(stream)
                left.append(stream)
            except StopIteration:
                pass
        streams = left


def ring_gather(links, along, here, view):
    before, after = lax.rem(here + 3, SIDE), lax.rem(here + 1, SIDE)
    own = view(here, None)
    right = links.copy(own, own, along(1))
    left = links.copy(own, own, along(3))
    yield
    right.wait_recv()
    passed = view(before, 0)
    onward = links.copy(passed, passed, along(1))
    left.wait_recv()
    passed = view(after, 1)
    back = links.copy(passed, passed, along(3))
    yield
    onward.wait_recv()
    back.wait_recv()


def both(first, second):
    done = object()
    while True:
        a, b = next(first, done), next(second, done)
        if a is done and b is done:
            return
        yield


def line_gather(links, source, place, local_sem):
    local = pltpu.make_async_copy(source, place, local_sem)
    local.start()
    copies = [links.copy(source, place, links.along_z(k)) for k in (1, 3, 2)]
    yield
    for made in copies:
        made.wait_recv()
    local.wait()


def halves(index_of):
    def view(i, h):
        return index_of(i, slice(None) if h is None else pl.ds(2 * h, 2))

    return view


def gather_weight(links, source, full, local_sem):
    y, x, z = links.y, links.x, links.z
    yield from line_gather(links, source, full.at[y, x, z], local_sem)
    yield from both(
        ring_gather(links, links.along_x, x, halves(lambda i, part: full.at[y, i, part, 0])),
        ring_gather(links, links.along_y, y, halves(lambda i, part: full.at[i, x, part, 1])),
    )
    yield from both(
        ring_gather(links, links.along_y, y, halves(lambda i, part: full.at[i, part, :, 0])),
        ring_gather(links, links.along_x, x, halves(lambda i, part: full.at[part, i, :, 1])),
    )


def gather_weights_kernel(w_qkv, w_out, full_qkv, full_out, send, recv, local):
    links = Links(send, recv)
    links.greet(
        [links.along_z(k) for k in (1, 2, 3)]
        + [links.along_x(1), links.along_x(3), links.along_y(1), links.along_y(3)]
    )
    interleave(
        [
            gather_weight(links, w_qkv, full_qkv, local.at[0]),
            gather_weight(links, w_out, full_out, local.at[1]),
        ]
    )
    links.finish()


def gather_rows_kernel(rows, full, send, recv, local):
    links = Links(send, recv)
    links.greet([links.along_z(k) for k in (1, 2, 3)] + [links.along_x(1), links.along_x(3)])

    def stream():
        yield from line_gather(links, rows, full.at[links.x, links.z], local.at[0])
        yield from ring_gather(
            links, links.along_x, links.x, halves(lambda i, part: full.at[i, part])
        )

    interleave([stream()])
    links.finish()


def add_blocks(target, *terms):
    first, second = target.shape[0], target.shape[1]

    def step(i, carry):
        at = (i // second, i % second)
        total = terms[0][at].astype(jnp.float32)
        for term in terms[1:]:
            total = total + term[at].astype(jnp.float32)
        target[at] = total.astype(target.dtype)
        return carry

    lax.fori_loop(0, first * second, step, 0)


def ring_sum(links, along, here, view, result, scratch):
    passing, from_left, from_right = scratch
    left, right, across = (
        lax.rem(here + 3, SIDE),
        lax.rem(here + 1, SIDE),
        lax.rem(here + 2, SIDE),
    )
    first = links.copy(view(across, 0), passing.at[0], along(1))
    second = links.copy(view(across, 1), passing.at[1], along(3))
    plain_right = links.copy(view(right, 1), from_left.at[1], along(1))
    plain_left = links.copy(view(left, 0), from_right.at[0], along(3))
    yield
    first.wait_recv()
    add_blocks(passing.at[0], passing.at[0], view(right, 0))
    summed_right = links.copy(passing.at[0], from_left.at[0], along(1))
    second.wait_recv()
    add_blocks(passing.at[1], passing.at[1], view(left, 1))
    summed_left = links.copy(passing.at[1], from_right.at[1], along(3))
    yield
    plain_left.wait_recv()
    summed_right.wait_recv()
    add_blocks(result(0), view(here, 0), from_left.at[0], from_right.at[0])
    plain_right.wait_recv()
    summed_left.wait_recv()
    add_blocks(result(1), view(here, 1), from_left.at[1], from_right.at[1])


def line_sum(links, terms, result, arrived):
    copies = [
        links.copy(terms.at[lax.rem(links.z + k, SIDE)], arrived.at[k - 1], links.along_z(k))
        for k in (1, 3, 2)
    ]
    yield
    for made in copies:
        made.wait_recv()
    own = terms.at[links.z]
    rows = 32

    def step(i, carry):
        at = (i // (own.shape[1] // rows), pl.ds(i % (own.shape[1] // rows) * rows, rows))
        total = own[at].astype(jnp.float32)
        for k in range(3):
            total = total + arrived[(k,) + at].astype(jnp.float32)
        result[at] = total.astype(result.dtype)
        return carry

    lax.fori_loop(0, own.shape[0] * (own.shape[1] // rows), step, 0)


def sum_weight(links, terms, result, scratch):
    ring_ya, ring_xb, mid_a, mid_b, ring_xa, ring_yb, last, arrived = scratch
    y, x = links.y, links.x
    yield from both(
        ring_sum(
            links, links.along_y, y,
            lambda i, h: terms.at[i, pl.ds(2 * h, 2), :, 0],
            lambda h: mid_a.at[pl.ds(2 * h, 2)], ring_ya,
        ),
        ring_sum(
            links, links.along_x, x,
            lambda i, h: terms.at[pl.ds(2 * h, 2), i, :, 1],
            lambda h: mid_b.at[pl.ds(2 * h, 2)], ring_xb,
        ),
    )
    yield from both(
        ring_sum(
            links, links.along_x, x,
            lambda i, h: mid_a.at[pl.ds(i, 1), pl.ds(2 * h, 2)],
            lambda h: last.at[pl.ds(0, 1), pl.ds(2 * h, 2), 0], ring_xa,
        ),
        ring_sum(
            links, links.along_y, y,
            lambda i, h: mid_b.at[pl.ds(i, 1), pl.ds(2 * h, 2)],
            lambda h: last.at[pl.ds(0, 1), pl.ds(2 * h, 2), 1], ring_yb,
        ),
    )
    yield from line_sum(links, last.at[0], result, arrived)


def sum_weight_scratch(columns):
    def vmem(*shape):
        return pltpu.VMEM(shape + (32, columns), jnp.bfloat16)

    big = (vmem(2, 2, 4), vmem(2, 2, 4), vmem(2, 2, 4))
    small = (vmem(2, 1, 2), vmem(2, 1, 2), vmem(2, 1, 2))
    return (big, big, vmem(4, 4), vmem(4, 4), small, small, vmem(1, 4, 2), vmem(3, 2))


def sum_rows(links, terms, result, scratch):
    ring, middle, arrived = scratch
    yield from ring_sum(
        links, links.along_x, links.x,
        lambda i, h: terms.at[pl.ds(i, 1), pl.ds(2 * h, 2)],
        lambda h: middle.at[pl.ds(0, 1), pl.ds(2 * h, 2), 0], ring,
    )
    yield from line_sum(links, middle.at[0], result, arrived)


def sum_rows_scratch(rows, columns):
    def vmem(*shape):
        return pltpu.VMEM(shape + (rows, columns), jnp.bfloat16)

    small = (vmem(2, 1, 2), vmem(2, 1, 2), vmem(2, 1, 2))
    return (small, pltpu.VMEM((1, 4, 1, rows, columns), jnp.bfloat16), pltpu.VMEM((3, 1, rows, columns), jnp.bfloat16))


def sum_groups(links, terms, result, scratch):
    near, pair, far = scratch
    width = result.shape[1]
    core = lax.rem(links.t, 2)
    side = links.t // 2

    def columns(owner):
        return pl.ds(pl.multiple_of(owner * width, width), width)

    far_owner = (1 - side) * 2
    near_owner = side * 2
    first = links.copy(
        terms.at[:, columns(far_owner + 1 - core)], near.at[0], links.other_core()
    )
    second = links.copy(
        terms.at[:, columns(near_owner + 1 - core)], near.at[1], links.other_core()
    )
    yield
    first.wait_recv()
    rows = 16
    steps = result.shape[0] // rows

    def pair_step(i, carry):
        at = pl.ds(i * rows, rows)
        total = terms[at, columns(far_owner + core)].astype(jnp.float32) + near[0, at].astype(
            jnp.float32
        )
        pair[at] = total.astype(pair.dtype)
        return carry

    lax.fori_loop(0, steps, pair_step, 0)
    across = links.copy(pair, far, links.other_side())
    yield
    yield
    yield
    second.wait_recv()
    across.wait_recv()

    def last_step(i, carry):
        at = pl.ds(i * rows, rows)
        total = terms[at, columns(near_owner + core)].astype(jnp.float32) + near[1, at].astype(
            jnp.float32
        )
        result[at] = (total + far[at].astype(jnp.float32)).astype(result.dtype)
        return carry

    lax.fori_loop(0, steps, last_step, 0)


def sum_groups_scratch(rows, width):
    return (
        pltpu.VMEM((2, rows, width), jnp.bfloat16),
        pltpu.VMEM((rows, width), jnp.bfloat16),
        pltpu.VMEM((rows, width), jnp.bfloat16),
    )


def all_partners(links):
    return (
        [links.along_z(k) for k in (1, 2, 3)]
        + [links.along_x(1), links.along_x(3), links.along_y(1), links.along_y(3)]
        + [links.other_core(), links.other_side()]
    )


def middle_sums_kernel(kv_terms, group_terms, weight_terms, kv_sum, group_sum, weight_sum, scratch, send, recv):
    links = Links(send, recv)
    links.greet(all_partners(links))
    interleave(
        [
            sum_rows(links, kv_terms, kv_sum, scratch[0]),
            sum_groups(links, group_terms, group_sum, scratch[1]),
            sum_weight(links, weight_terms, weight_sum, scratch[2]),
        ]
    )
    links.finish()


def last_sums_kernel(group_terms, weight_terms, group_sum, weight_sum, scratch, send, recv):
    links = Links(send, recv)
    links.greet(all_partners(links))
    interleave(
        [
            sum_groups(links, group_terms, group_sum, scratch[0]),
            sum_weight(links, weight_terms, weight_sum, scratch[1]),
        ]
    )
    links.finish()


def attention_kernel(query_pos, key_pos, queries, head_grads, kv, heads_out, query_grad, kv_grad, totals):
    score_scale = HD ** (-0.5)
    keys, values = kv[:, :HD], kv[:, HD:]
    keys_t, values_t = keys.T, values.T
    rows = 256
    last = (((1,), (1,)), ((), ()))
    totals[...] = jnp.zeros_like(totals)

    def step(i, carry):
        at = pl.ds(i * rows, rows)
        q, grads = queries[at], head_grads[at]
        allowed = key_pos[...] <= query_pos[...]
        scores = lax.dot_general(keys, q, last, preferred_element_type=jnp.float32) * score_scale
        scores = jnp.where(allowed, scores, masked_score)
        row_max = jnp.max(scores, axis=0, keepdims=True)
        raw = jnp.where(allowed, jnp.exp(scores - row_max), 0.0)
        row_sum = jnp.sum(raw, axis=0, keepdims=True)
        weighted = jnp.dot(values_t, raw.astype(jnp.bfloat16), preferred_element_type=jnp.float32)
        out = (weighted / row_sum).astype(jnp.bfloat16)
        out_rows = out.astype(jnp.float32).T
        row_dots = jnp.sum(grads.astype(jnp.float32).T * out.astype(jnp.float32), axis=0, keepdims=True)
        weights = raw * (1.0 / row_sum)
        dweights = lax.dot_general(values, grads, last, preferred_element_type=jnp.float32)
        dscores = (weights * (dweights - row_dots)).astype(jnp.bfloat16)
        heads_out[at] = out_rows.astype(jnp.bfloat16)
        dq = jnp.dot(keys_t, dscores, preferred_element_type=jnp.float32)
        query_grad[at] = dq.T * score_scale
        totals[:, :HD] += jnp.dot(dscores, q, preferred_element_type=jnp.float32) * score_scale
        totals[:, HD:] += jnp.dot(weights.astype(jnp.bfloat16), grads, preferred_element_type=jnp.float32)
        return carry

    lax.fori_loop(0, queries.shape[0] // rows, step, 0)
    kv_grad[...] = totals[...].astype(jnp.bfloat16)


VMEM = pl.BlockSpec(memory_space=pltpu.VMEM)
HBM = pl.BlockSpec(memory_space=pl.ANY)


def call(kernel, outs, ins, in_specs, out_specs, scratch, identity=None, copies=0, limit=40):
    if copies:
        scratch = list(scratch) + [pltpu.SemaphoreType.DMA((copies,))] * 2
    return pl.pallas_call(
        kernel,
        out_shape=outs,
        in_specs=in_specs,
        out_specs=out_specs,
        scratch_shapes=scratch,
        compiler_params=pltpu.CompilerParams(
            collective_id=identity,
            has_side_effects=identity is not None,
            vmem_limit_bytes=limit * 2**20,
        ),
    )(*ins)


def shape(dims, kind=jnp.bfloat16):
    return jax.ShapeDtypeStruct(dims, kind)


def body(normed, w_qkv, w_out, block_order, d_out):
    local_rows = normed.shape[1]
    block_rows = local_rows // 2
    model = normed.shape[2]
    q_width = w_out.shape[1]
    qkv_width = w_qkv.shape[1]
    head_count = q_width // HD
    ctx_count = lax.axis_size("ctx")
    length = local_rows * ctx_count
    ctx_index = lax.axis_index("ctx")
    query_pos = stored_positions(
        block_order, ctx_index * local_rows + jnp.arange(local_rows, dtype=jnp.int32), block_rows
    )
    all_pos = stored_positions(block_order, jnp.arange(length, dtype=jnp.int32), block_rows)

    full_qkv, full_out = pl.pallas_call(
        gather_weights_kernel,
        out_shape=[shape((4, 4, 4, 2, 32, qkv_width)), shape((4, 4, 4, 2, 32, q_width))],
        in_specs=[HBM, HBM],
        out_specs=[HBM, HBM],
        scratch_shapes=[
            pltpu.SemaphoreType.DMA((38,)),
            pltpu.SemaphoreType.DMA((38,)),
            pltpu.SemaphoreType.DMA((2,)),
        ],
        compiler_params=pltpu.CompilerParams(collective_id=1, has_side_effects=True),
    )(w_qkv.reshape(2, 32, qkv_width), w_out.reshape(2, 32, q_width))
    qkv_weight = full_qkv.reshape(model, qkv_width)
    out_weight = full_out.reshape(model, q_width)

    tokens = normed[0]
    upstream = d_out[0]
    projected = jnp.dot(tokens, qkv_weight, preferred_element_type=jnp.float32)
    cosine, sines = rope_tables(query_pos, HD)
    turned = apply_rope(
        projected[:, : q_width + HD].reshape(local_rows, head_count + 1, HD), cosine, sines, 1.0
    ).astype(jnp.bfloat16)
    kv = jnp.concatenate(
        [turned[:, head_count], projected[:, q_width + HD :].astype(jnp.bfloat16)], axis=1
    )
    full_kv = pl.pallas_call(
        gather_rows_kernel,
        out_shape=shape((4, 4, local_rows, 2 * HD)),
        in_specs=[HBM],
        out_specs=HBM,
        scratch_shapes=[
            pltpu.SemaphoreType.DMA((7,)),
            pltpu.SemaphoreType.DMA((7,)),
            pltpu.SemaphoreType.DMA((1,)),
        ],
        compiler_params=pltpu.CompilerParams(collective_id=2, has_side_effects=True),
    )(kv).reshape(length, 2 * HD)

    head_grads = jnp.dot(upstream, out_weight, preferred_element_type=jnp.float32).astype(
        jnp.bfloat16
    )

    def by_head(rows):
        return jnp.transpose(rows.reshape(local_rows, head_count, HD), (1, 0, 2)).reshape(
            head_count * local_rows, HD
        )

    def by_row(heads):
        return jnp.transpose(heads.reshape(head_count, local_rows, HD), (1, 0, 2)).reshape(
            local_rows, q_width
        )

    stacked = head_count * local_rows
    heads_out, query_grad, kv_terms = call(
        attention_kernel,
        [
            shape((stacked, HD)),
            shape((stacked, HD), jnp.float32),
            shape((length, 2 * HD)),
        ],
        [
            jnp.concatenate([query_pos, query_pos])[None, :],
            all_pos[:, None],
            by_head(turned[:, :head_count].reshape(local_rows, q_width)),
            by_head(head_grads),
            full_kv,
        ],
        [VMEM] * 5,
        [VMEM] * 3,
        [pltpu.VMEM((length, 2 * HD), jnp.float32)],
    )
    heads_out = by_row(heads_out)
    out_term = lax.dot_general(
        heads_out, out_weight, (((1,), (1,)), ((), ())), preferred_element_type=jnp.float32
    ).astype(jnp.bfloat16)
    out_weight_term = lax.dot_general(
        upstream, heads_out, (((0,), (0,)), ((), ())), preferred_element_type=jnp.float32
    ).astype(jnp.bfloat16)
    width = model // 4
    kv_sum, attn_out, d_w_out = call(
        middle_sums_kernel,
        [
            shape((1, local_rows, 2 * HD), jnp.float32),
            shape((local_rows, width)),
            shape((2, 32, q_width)),
        ],
        [
            kv_terms.reshape(4, 4, local_rows, 2 * HD),
            out_term,
            out_weight_term.reshape(4, 4, 4, 2, 32, q_width),
        ],
        [VMEM] * 3,
        [VMEM] * 3,
        [
            (
                sum_rows_scratch(local_rows, 2 * HD),
                sum_groups_scratch(local_rows, width),
                sum_weight_scratch(q_width),
            )
        ],
        identity=3,
        copies=9 + 3 + 27,
    )
    rotated = apply_rope(
        jnp.concatenate([by_row(query_grad), kv_sum[0, :, :HD]], axis=1).reshape(
            local_rows, head_count + 1, HD
        ),
        cosine,
        sines,
        -1.0,
    )
    qkv_grads = jnp.concatenate(
        [rotated.reshape(local_rows, q_width + HD), kv_sum[0, :, HD:]], axis=1
    ).astype(jnp.bfloat16)
    input_term = lax.dot_general(
        qkv_grads, qkv_weight, (((1,), (1,)), ((), ())), preferred_element_type=jnp.float32
    ).astype(jnp.bfloat16)
    qkv_weight_term = lax.dot_general(
        tokens, qkv_grads, (((0,), (0,)), ((), ())), preferred_element_type=jnp.float32
    ).astype(jnp.bfloat16)
    d_normed, d_w_qkv = call(
        last_sums_kernel,
        [shape((local_rows, width)), shape((2, 32, qkv_width))],
        [input_term, qkv_weight_term.reshape(4, 4, 4, 2, 32, qkv_width)],
        [VMEM] * 2,
        [VMEM] * 2,
        [(sum_groups_scratch(local_rows, width), sum_weight_scratch(qkv_width))],
        identity=4,
        copies=3 + 27,
    )
    return (
        attn_out[None],
        d_normed[None],
        d_w_qkv.reshape(w_qkv.shape),
        d_w_out.reshape(w_out.shape),
    )


def solution(mesh):
    in_specs = (
        P("dp", "ctx", None),
        P(("dp", "ctx"), "tp"),
        P(("dp", "ctx"), "tp"),
        P(),
        P("dp", "ctx", None),
    )
    out_specs = (
        P("dp", "ctx", "tp"),
        P("dp", "ctx", "tp"),
        P(("dp", "ctx"), "tp"),
        P(("dp", "ctx"), "tp"),
    )
    return jax.shard_map(body, mesh=mesh, in_specs=in_specs, out_specs=out_specs, check_vma=False)
```

time: 1440 us -> 254 us (0.18)
  waiting for transfers between devices: 1250 us -> 0 us
  Pallas kernels: 0 us -> 191 us
  blocking collectives: 83.6 us -> 0 us
  matrix products: 52.4 us -> 25.1 us
  local copies, waits for them, and re-layouts: 13.1 us -> 29.1 us
    all_gather x2 -> x0, waiting for transfers between devices: 721 us -> none  [the longest x1 363 us: body(): lax.all_gather(w_qkv, ('dp', 'ctx'), axis=0, tiled=True)]
    reduce_scatter x6 -> x0, waiting for transfers between devices: 353 us -> none  [the longest x1 80.7 us: body(): lax.psum_scatter(value_grad_all.astype(jnp.bfloat16), 'ctx', scatter_dime...]
    pallas_call x0 -> x5, Pallas kernels: none -> 191 us  [the longest x3 97.5 us: call(): pl.pallas_call(kernel, out_shape=outs, in_specs=in_specs, out_specs=out_s...]
    unnamed x12 -> x0, waiting for transfers between devices: 173 us -> none
    all_gather x2 -> x0, blocking collectives: 83.6 us -> none  [the longest x1 43.9 us: body(): lax.all_gather(value_rows, 'ctx', axis=0, tiled=True)]
    dot_general x28 -> x4, matrix products: 45.4 us -> 17.6 us  [the longest x1 4.96 us: body(): lax.dot_general(qkv_grads, qkv_weight, (((1,), (1,)), ((), ())), preferre...]
    convert_element_type x0 -> x2, local copies, waits for them, and re-layouts: none -> 15.1 us  [the longest x1 8.63 us: body(): qkv_weight_term = lax.dot_general(tokens, qkv_grads, (((0,), (0,)), ((),...]
  transfers between devices with their start and end apart: 10 -> 0, of which waited for: 10 -> 0; matrix products, arithmetic and copies ran while one was open for 2% -> 0% of each run, Pallas kernels for 0% -> 0%
where the time goes in v1:
time: 254 us; the launch traced here: 252 us
  Pallas kernels  191 us (75%)
  local copies, waits for them, and re-layouts  29.1 us (11%)
  matrix products  25.1 us (10%)
  other arithmetic  6 us (2%)
    pallas_call x3, Pallas kernels, call(): pl.pallas_call(kernel, out_shape=outs, in_specs=in_specs, out_specs=out_s...  97.5 us
    pallas_call x1, Pallas kernels, body(): pl.pallas_call(gather_weights_kernel, out_shape=[shape((4, 4, 4, 2, 32, q...  70.2 us
    pallas_call x1, Pallas kernels, body(): pl.pallas_call(gather_rows_kernel, out_shape=shape((4, 4, local_rows, 2 *...  23.7 us
    unnamed x17, local copies, waits for them, and re-layouts  10.3 us
    convert_element_type x1, local copies, waits for them, and re-layouts, body(): qkv_weight_term = lax.dot_general(tokens, qkv_grads, (((0,), (0,)), ((),...  8.63 us
    convert_element_type x1, local copies, waits for them, and re-layouts, body(): out_weight_term = lax.dot_general(upstream, heads_out, (((0,), (0,)), (()...  6.47 us

profile of v1, /device:TPU:64, one launch (start us, length us, event | category | flops | bytes accessed | tf_op | source)
XLA Modules:
  0.0 252.5 jit_solution(1854099606094643142)
XLA Ops:
  0.6 0.0 copy-start
  0.7 0.8 select_reduce_fusion.1
  1.5 0.8 select_reduce_fusion
  2.3 0.1 broadcast_multiply_fusion.1
  2.4 0.3 broadcast_multiply_fusion
  2.7 0.7 copy.43
  3.5 0.7 copy.47
  4.2 0.4 copy.31
  4.6 0.1 fusion.2.key_pos
  4.7 70.2 %shard_map.84 = (bf16[4,4,4,2,32,768]{5,4,3,2,1,0:T(8,128)(2,1)}, bf16[4,4,4,2,32,512]{5,4,3,2,1,0:T(8,128)(2,1)}) custom-call(bf16[2,32,768]{2,1,0:T(8,128)(2,1)} %bitcast.93, bf16[2,32,512]{2,1,0:T(8,128)(2,1)} %bitcast.94), custom_call_target="tpu_custom_call" | custom-call | tf_op jit(solution)/shard_map/pallas_call | solution.py:472
  74.8 3.8 %convolution_convert_fusion.4 = bf16[512,128]{1,0:T(8,128)(2,1)S(1)} fusion(bf16[4096,512]{1,0:T(8,128)(2,1)} %bitcast.84, bf16[1,128,4096]{2,1,0:T(8,128)(2,1)} %param.9), kind=kOutput, calls=%fused_computation.8 | convolution fusion | flops 536936448 | bytes 5373952 | tf_op jit(solution)/shard_map/dot_general | solution.py:510
  78.6 0.1 copy.37
  78.8 0.0 copy-done
  78.8 3.8 %convolution_bitcast_fusion = f32[128,768]{1,0:T(8,128)S(1)} fusion(bf16[4096,768]{1,0:T(8,128)(2,1)} %bitcast.82, bf16[1,128,4096]{2,1,0:T(8,128)(2,1)S(1)} %copy-done), kind=kOutput, calls=%fused_computation.7 | convolution fusion | flops 805306368 | bytes 7733248 | tf_op jit(solution)/shard_map/dot_general | solution.py:489
  82.6 0.2 copy.33
  82.8 0.2 copy.34
  82.9 0.2 slice_negate_fusion
  83.1 0.2 fusion.11
  83.3 0.6 pad_maximum_fusion.5.rows
  83.9 23.7 %shard_map.85 = bf16[4,4,128,256]{3,2,1,0:T(8,128)(2,1)} custom-call(bf16[128,256]{1,0:T(8,128)(2,1)} %pad_maximum_fusion.5.rows), custom_call_target="tpu_custom_call" | custom-call | tf_op jit(solution)/shard_map/pallas_call | solution.py:497
  107.6 0.0 copy-start.3
  107.6 1.2 copy-done.3
  108.8 6.0 %shard_map.86 = (bf16[512,128]{1,0:T(8,128)(2,1)S(1)}, f32[512,128]{1,0:T(8,128)S(1)}, bf16[2048,256]{1,0:T(8,128)(2,1)S(1)}) custom-call(s32[1,256]{1,0:T(1,128)S(1)} %bitcast.81, s32[2048,1]{1,0:T(8,128)S(1)} %fusion.2.key_pos, bf16[512,128]{1,0:T(8,128)(2,1)S(1)} %bitcast.74, bf16[512,128]{1,0:T(8,128)(2,1)S(1)} %bitcast.73, bf16[2048,256]{1,0:T(8,128)(2,1)S(1)} %bitcast.71), custom_call_target="tpu_custom_call" | custom-call | tf_op jit(solution)/shard_map/pallas_call | solution.py:439
  114.9 0.0 copy-start.4
  114.9 0.7 copy-done.4
  115.6 0.1 copy.38
  115.7 3.7 %convolution_convert_fusion.3.group_terms = bf16[128,4096]{1,0:T(8,128)(2,1)S(1)} fusion(bf16[128,512]{0,1:T(8,128)(2,1)S(1)} %bitcast.88, bf16[4096,512]{1,0:T(8,128)(2,1)} %bitcast.85), kind=kOutput, calls=%fused_computation.5 | convolution fusion | flops 537395200 | bytes 5373952 | tf_op jit(solution)/shard_map/dot_general | solution.py:544
  119.4 1.8 copy.40
  121.2 4.5 %fusion.1 = bf16[4096,512]{0,1:T(8,128)(2,1)} fusion(bf16[128,512]{0,1:T(8,128)(2,1)S(1)} %bitcast.89, bf16[1,128,4096]{2,1,0:T(8,128)(2,1)} %param.9), kind=kOutput, calls=%fused_computation.3 | convolution fusion | flops 538968064 | bytes 5373952 | tf_op jit(solution)/shard_map/dot_general | solution.py:547
  125.7 6.5 %copy.39 = bf16[4096,512]{1,0:T(8,128)(2,1)} copy(bf16[4096,512]{0,1:T(8,128)(2,1)} %fusion.1) | data formatting | bytes 8388608 | tf_op jit(solution)/shard_map/convert_element_type | solution.py:549
  132.2 0.0 copy-start.2
  132.2 2.2 copy-done.2
  134.3 43.8 %shard_map.87 = (f32[1,128,256]{2,1,0:T(8,128)S(1)}, bf16[128,1024]{1,0:T(8,128)(2,1)S(1)}, bf16[2,32,512]{2,1,0:T(8,128)(2,1)S(1)}) custom-call(bf16[4,4,128,256]{3,2,1,0:T(8,128)(2,1)S(1)} %bitcast.72, bf16[128,4096]{1,0:T(8,128)(2,1)S(1)} %convolution_convert_fusion.3.group_terms, bf16[4,4,4,2,32,512]{5,4,3,2,1,0:T(8,128)(2,1)S(1)} %bitcast.70), custom_call_target="tpu_custom_call" | custom-call | tf_op jit(solution)/shard_map/pallas_call | solution.py:439
  178.2 0.1 copy.41
  178.3 0.1 copy.44
  178.4 1.0 pad_maximum_fusion
  179.4 0.9 maximum_multiply_fusion.1
  180.3 0.0 copy-done.5
  180.3 1.0 fusion.12
  181.3 5.0 %convolution_convert_fusion.2.group_terms = bf16[128,4096]{1,0:T(8,128)(2,1)S(1)} fusion(bf16[4096,768]{1,0:T(8,128)(2,1)} %bitcast.83, bf16[128,128]{0,1:T(8,128)(2,1)S(1)} %copy.44, bf16[128,640]{0,1:T(8,128)(2,1)S(1)} %fusion.12), kind=kOutput, calls=%fused_computation.4 | convolution fusion | flops 806223872 | bytes 7536640 | tf_op jit(solution)/shard_map/dot_general | solution.py:586
  186.3 4.5 %fusion = bf16[4096,768]{0,1:T(8,128)(2,1)} fusion(bf16[1,128,4096]{2,1,0:T(8,128)(2,1)S(1)} %copy-done, bf16[128,128]{0,1:T(8,128)(2,1)S(1)} %copy.44, bf16[128,640]{0,1:T(8,128)(2,1)S(1)} %fusion.12), kind=kOutput, calls=%fused_computation.2 | convolution fusion | flops 808845312 | bytes 7536640 | tf_op jit(solution)/shard_map/dot_general | solution.py:589
  190.7 8.6 %copy.45 = bf16[4096,768]{1,0:T(8,128)(2,1)} copy(bf16[4096,768]{0,1:T(8,128)(2,1)} %fusion) | data formatting | bytes 12582912 | tf_op jit(solution)/shard_map/convert_element_type | solution.py:591
  199.4 2.8 %copy-done.1 = bf16[4096,768]{1,0:T(8,128)(2,1)S(1)} copy-done((bf16[4096,768]{1,0:T(8,128)(2,1)S(1)}, bf16[4096,768]{1,0:T(8,128)(2,1)}, u32[]{:S(2)}) %copy-start.1) | copy-done | bytes 6291480
  202.2 47.6 %shard_map.88 = (bf16[128,1024]{1,0:T(8,128)(2,1)S(1)}, bf16[2,32,768]{2,1,0:T(8,128)(2,1)S(1)}) custom-call(bf16[128,4096]{1,0:T(8,128)(2,1)S(1)} %convolution_convert_fusion.2.group_terms, bf16[4,4,4,2,32,768]{5,4,3,2,1,0:T(8,128)(2,1)S(1)} %bitcast.69), custom_call_target="tpu_custom_call" | custom-call | tf_op jit(solution)/shard_map/pallas_call | solution.py:439
  249.8 0.7 copy.52
  250.5 0.7 copy.53
  251.2 0.6 copy.54
  251.9 0.6 copy.55
  (15 shorter events, 0.1 us)
Async XLA Ops:
  0.6 78.1 %copy-start = (bf16[1,128,4096]{2,1,0:T(8,128)(2,1)S(1)}, bf16[1,128,4096]{2,1,0:T(8,128)(2,1)}, u32[]{:S(2)}) copy-start(bf16[1,128,4096]{2,1,0:T(8,128)(2,1)} %param.5) | copy-start | bytes 3145732
  107.6 1.2 copy-start.3
  114.9 0.7 copy-start.4
  132.2 2.2 copy-start.2
  134.3 46.0 %copy-start.5 = (f32[128,128]{0,1:T(8,128)S(1)}, f32[128,128]{0,1:T(8,128)}, u32[]{:S(2)}) copy-start(f32[128,128]{0,1:T(8,128)} %copy.47) | copy-start | bytes 196612
  199.4 2.8 %copy-start.1 = (bf16[4096,768]{1,0:T(8,128)(2,1)S(1)}, bf16[4096,768]{1,0:T(8,128)(2,1)}, u32[]{:S(2)}) copy-start(bf16[4096,768]{1,0:T(8,128)(2,1)} %copy.45) | copy-start | bytes 18874372

commit v2 on v1

v2 whole, which is shorter than its diff:
```python
import jax
import jax.numpy as jnp
from jax import lax
from jax.experimental import pallas as pl
from jax.experimental.pallas import tpu as pltpu
from jax.sharding import PartitionSpec as P

HD = 128
SIDE = 4
MESH = pl.DeviceIdType.MESH

rope_base = 500000.0
masked_score = -1e30
contract_last = (((1,), (1,)), ((), ()))
contract_first = (((0,), (0,)), ((), ()))


def stored_positions(order, row_ids, block_rows):
    owner = row_ids // block_rows
    matches = owner[:, None] == jnp.arange(order.shape[0], dtype=jnp.int32)[None, :]
    picked = jnp.sum(jnp.where(matches, order[None, :], 0), axis=1)
    return picked * block_rows + row_ids % block_rows


def rope_tables(positions, head_size):
    half_size = head_size // 2
    frequency = rope_base ** (-2.0 * jnp.arange(half_size, dtype=jnp.float32) / head_size)
    angles = positions.astype(jnp.float32)[:, None] * frequency[None, :]
    sines = jnp.sin(angles)
    cosine = jnp.cos(angles)
    return (
        jnp.concatenate([cosine, cosine], axis=1),
        jnp.concatenate([-sines, sines], axis=1),
    )


def swap_halves(values):
    half_size = values.shape[-1] // 2
    return jnp.concatenate([values[..., half_size:], values[..., :half_size]], axis=-1)


class Links:
    def __init__(self, send, recv):
        self.send, self.recv, self.used, self.copies = send, recv, 0, []
        self.y = lax.axis_index("dp")
        self.c = lax.axis_index("ctx")
        self.t = lax.axis_index("tp")
        self.x = self.c // SIDE
        self.z = self.c % SIDE
        self.core = lax.rem(self.t, 2)
        self.side = self.t // 2

    def along_y(self, k):
        return (lax.rem(self.y + k, SIDE), self.c, self.t)

    def along_x(self, k):
        return (self.y, lax.rem(self.x + k, SIDE) * SIDE + self.z, self.t)

    def along_z(self, k):
        return (self.y, self.x * SIDE + lax.rem(self.z + k, SIDE), self.t)

    def other_core(self):
        return (self.y, self.c, self.t + 1 - 2 * self.core)

    def other_side(self):
        return (self.y, self.c, lax.rem(self.t + 2, 4))

    def greet(self, sides=False):
        partners = (
            [self.along_y(k) for k in (1, 2, 3)]
            + [self.along_z(k) for k in (1, 2, 3)]
            + [self.along_x(1), self.along_x(3), self.other_core()]
        )
        if sides:
            partners.append(self.other_side())
        barrier = pltpu.get_barrier_semaphore()
        for partner in partners:
            pl.semaphore_signal(barrier, inc=1, device_id=partner, device_id_type=MESH)
        pl.semaphore_wait(barrier, len(partners))

    def copy(self, source, target, partner):
        made = pltpu.make_async_remote_copy(
            src_ref=source,
            dst_ref=target,
            send_sem=self.send.at[self.used],
            recv_sem=self.recv.at[self.used],
            device_id=partner,
            device_id_type=MESH,
        )
        made.start()
        self.used += 1
        self.copies.append(made)
        return made

    def finish(self):
        for made in self.copies:
            made.wait_send()


def local_copy(source, target, semaphore):
    made = pltpu.make_async_copy(source, target, semaphore)
    made.start()
    return made


def in_order(streams, order):
    for name in order:
        next(streams[name], None)
    for stream in streams.values():
        for _ in stream:
            pass


def column(i, width=HD):
    return pl.ds(pl.multiple_of(i * width, width), width)


def ring_gather(links, along, here, view, source=None, arrived=None):
    before, after, across = (
        lax.rem(here + 3, SIDE),
        lax.rem(here + 1, SIDE),
        lax.rem(here + 2, SIDE),
    )
    arrived = arrived or (lambda block: None)
    own = view(here, None)
    source = own if source is None else source
    right = links.copy(source, own, along(1))
    left = links.copy(source, own, along(3))
    yield
    right.wait_recv()
    passed = view(before, 0)
    onward = links.copy(passed, passed, along(1))
    left.wait_recv()
    passed = view(after, 1)
    back = links.copy(passed, passed, along(3))
    arrived(view(before, None))
    arrived(view(after, None))
    yield
    onward.wait_recv()
    arrived(view(across, 0))
    back.wait_recv()
    arrived(view(across, 1))


def gather_columns(links, source, chosen, full):
    y, x, z = links.y, links.x, links.z
    place = full.at[y, x, z]
    copies = [
        links.copy(source.at[:, column(chosen(lax.rem(y + k, SIDE)))], place, links.along_y(k))
        for k in (2, 1, 3)
    ]
    yield
    for made in copies:
        made.wait_recv()
    block = full.at[:, x, z]
    copies = [links.copy(block, block, links.along_z(k)) for k in (2, 1, 3)]
    yield
    for made in copies:
        made.wait_recv()
    yield from ring_gather(
        links,
        links.along_x,
        x,
        lambda i, h: full.at[:, i] if h is None else full.at[pl.ds(2 * h, 2), i],
    )


def gather_tokens(links, source, full):
    half = source.shape[0] // 2
    first = pl.multiple_of(links.core * half, half)
    handed = []

    def view(i, h):
        if h is None:
            return full.at[i, pl.ds(first, half)]
        return full.at[i, pl.ds(pl.multiple_of(first + h * (half // 2), half // 2), half // 2)]

    def hand(block):
        handed.append(links.copy(block, block, links.other_core()))

    yield from ring_gather(
        links, links.along_y, links.y, view, source.at[pl.ds(first, half)], hand
    )
    yield
    for made in handed:
        made.wait_recv()


def front_kernel(
    normed, d_out, w_qkv, w_out, all_normed, all_d_out, full_q, full_kv, full_out, held,
    send, recv, local,
):
    links = Links(send, recv)
    y, x, z = links.y, links.x, links.z
    heads = w_out.shape[1] // HD
    weights = {
        "q": (w_qkv, lambda j: j, full_q),
        "k": (w_qkv, lambda j: heads + lax.rem(j, 2), full_kv),
        "o": (w_out, lambda j: j, full_out),
    }
    mine = [
        local_copy(source.at[:, column(chosen(y))], full.at[y, x, z], local.at[i])
        for i, (source, chosen, full) in enumerate(weights.values())
    ]
    loads = [
        local_copy(source, held.at[i], local.at[3 + i]) for i, source in enumerate((normed, d_out))
    ]
    links.greet()
    for made in mine + loads:
        made.wait()
    streams = {name: gather_columns(links, *given) for name, given in weights.items()}
    streams["n"] = gather_tokens(links, held.at[0], all_normed)
    streams["d"] = gather_tokens(links, held.at[1], all_d_out)
    start = "qkon"
    for name in start:
        next(streams[name])
    kept = [
        local_copy(held.at[i], full.at[y], local.at[3 + i])
        for i, full in enumerate((all_normed, all_d_out))
    ]
    in_order(streams, "qkoqndknoqkdoqkdond")
    for made in kept:
        made.wait()
    links.finish()


def exchange_heads(links, source, place, own_semaphore):
    copies = [
        links.copy(source.at[lax.rem(links.y + k, SIDE)], place, links.along_y(k))
        for k in (2, 1, 3)
    ]
    return copies, local_copy(source.at[links.y], place, own_semaphore)


def middle_kernel(queries, grads, kv, all_queries, all_grads, all_kv, send, recv, local):
    links = Links(send, recv)
    y, x, z = links.y, links.x, links.z
    links.greet()
    place = all_kv.at[lax.rem(y, 2), x, z]
    passed = links.copy(kv.at[1], place, links.along_y(1))
    own = local_copy(kv.at[0], place, local.at[0])
    copies, mine = exchange_heads(links, queries, all_queries.at[y], local.at[1])
    more_copies, more_mine = exchange_heads(links, grads, all_grads.at[y], local.at[2])
    own.wait()
    passed.wait_recv()
    block = all_kv.at[:, x, z]
    for made in [links.copy(block, block, links.along_z(k)) for k in (2, 1, 3)]:
        made.wait_recv()
    for _ in ring_gather(
        links,
        links.along_x,
        x,
        lambda i, h: all_kv.at[:, i] if h is None else all_kv.at[pl.ds(h, 1), i],
    ):
        pass
    for made in copies + more_copies:
        made.wait_recv()
    mine.wait()
    more_mine.wait()
    links.finish()


def add_blocks(target, *terms):
    lead, (height, width) = target.shape[:-2], target.shape[-2:]
    rows = min(height, max(16, 16384 // width))
    per = height // rows
    count = per
    for size in lead:
        count *= size

    def step(i, carry):
        at = (pl.ds(pl.multiple_of(i % per * rows, rows), rows),)
        rest = i // per
        for size in lead[::-1]:
            at = (rest % size,) + at
            rest = rest // size
        total = terms[0][at].astype(jnp.float32)
        for term in terms[1:]:
            total = total + term[at].astype(jnp.float32)
        target[at] = total.astype(target.dtype)
        return carry

    lax.fori_loop(0, count, step, 0)


def ring_sum(links, along, here, view, result, scratch, prepare=None):
    passing, from_left, from_right = scratch
    left, right, across = (
        lax.rem(here + 3, SIDE),
        lax.rem(here + 1, SIDE),
        lax.rem(here + 2, SIDE),
    )
    prepare = prepare or (lambda i: None)
    prepare(across)
    first = links.copy(view(across, 0), passing.at[0], along(1))
    second = links.copy(view(across, 1), passing.at[1], along(3))
    prepare(right)
    plain_right = links.copy(view(right, 1), from_left.at[1], along(1))
    prepare(left)
    plain_left = links.copy(view(left, 0), from_right.at[0], along(3))
    yield
    prepare(here)
    first.wait_recv()
    add_blocks(passing.at[0], passing.at[0], view(right, 0))
    summed_right = links.copy(passing.at[0], from_left.at[0], along(1))
    second.wait_recv()
    add_blocks(passing.at[1], passing.at[1], view(left, 1))
    summed_left = links.copy(passing.at[1], from_right.at[1], along(3))
    yield
    plain_left.wait_recv()
    summed_right.wait_recv()
    add_blocks(result(0), view(here, 0), from_left.at[0], from_right.at[0])
    plain_right.wait_recv()
    summed_left.wait_recv()
    add_blocks(result(1), view(here, 1), from_left.at[1], from_right.at[1])


def sum_weight(links, tokens, grads, scratch):
    terms, ring, middle, arrived, summed, placed = scratch
    y, x, z = links.y, links.x, links.z
    size = 4 * terms.shape[3]

    def prepare(i):
        def step(owner, carry):
            at = column(owner * SIDE + i, size)
            rows = tokens[:, :, at].reshape(-1, size)
            part = lax.dot_general(
                rows,
                grads[...].reshape(rows.shape[0], HD),
                contract_first,
                preferred_element_type=jnp.float32,
            )
            terms[owner, i] = part.astype(jnp.bfloat16).reshape(terms.shape[2:])
            return carry

        lax.fori_loop(0, SIDE, step, 0)

    yield from ring_sum(
        links,
        links.along_x,
        x,
        lambda i, h: terms.at[pl.ds(2 * h, 2), i],
        lambda h: middle.at[pl.ds(2 * h, 2)],
        ring,
        prepare,
    )
    copies = [
        links.copy(middle.at[:, lax.rem(z + k, SIDE)], arrived.at[k - 1], links.along_z(k))
        for k in (2, 1, 3)
    ]
    yield
    for made in copies:
        made.wait_recv()
    add_blocks(summed, middle.at[:, z], arrived.at[0], arrived.at[1], arrived.at[2])
    copies = [
        links.copy(summed.at[lax.rem(y + k, SIDE)], placed.at[y], links.along_y(k))
        for k in (2, 1, 3)
    ]
    placed[y] = summed[y]
    yield
    for made in copies:
        made.wait_recv()


def sum_weight_scratch(rows):
    def vmem(*dims):
        return pltpu.VMEM(dims + (rows, HD), jnp.bfloat16)

    ring = (vmem(2, 2, 4), vmem(2, 2, 4), vmem(2, 2, 4))
    return (vmem(4, 4, 4), ring, vmem(4, 4), vmem(3, 4), vmem(4), vmem(4))


def sum_groups(links, rows, weight, result, scratch):
    terms, near, ring, paired, far = scratch
    width = result.shape[1]
    core, side = links.core, links.side
    size = 256

    def prepare(owner):
        def step(i, carry):
            part = lax.dot_general(
                rows[...].reshape(-1, rows.shape[2]),
                weight[pl.ds(pl.multiple_of(owner * width + i * size, size), size)],
                contract_last,
                preferred_element_type=jnp.float32,
            )
            terms[owner, :, :, column(i, size)] = part.astype(jnp.bfloat16).reshape(
                SIDE, rows.shape[1], size
            )
            return carry

        lax.fori_loop(0, width // size, step, 0)

    handed = []
    for i in range(2):
        prepare(2 * i + 1 - core)
        handed.append(links.copy(terms.at[2 * i + 1 - core], near.at[i], links.other_core()))
    for i in range(2):
        prepare(2 * i + core)
    yield
    for i in range(2):
        handed[i].wait_recv()
        add_blocks(terms.at[2 * i + core], terms.at[2 * i + core], near.at[i])
    yield from ring_sum(
        links,
        links.along_y,
        links.y,
        lambda i, h: terms.at[2 * h + core, i],
        lambda h: paired.at[h],
        ring,
    )
    across = links.copy(paired.at[1 - side], far, links.other_side())
    yield
    yield
    across.wait_recv()
    add_blocks(result, paired.at[side], far)


def sum_groups_scratch(rows, width):
    def vmem(*dims):
        return pltpu.VMEM(dims + (rows, width), jnp.bfloat16)

    return (vmem(4, 4), vmem(2, 4), (vmem(2), vmem(2), vmem(2)), vmem(2), vmem())


def sum_kv(links, terms, cosine, sines, grads, scratch):
    ring, middle, arrived, handed = scratch
    y, x, z = links.y, links.x, links.z
    yield from ring_sum(
        links,
        links.along_x,
        x,
        lambda i, h: terms.at[pl.ds(h, 1), i],
        lambda h: middle.at[pl.ds(h, 1)],
        ring,
    )
    copies = [
        links.copy(middle.at[:, lax.rem(z + k, SIDE)], arrived.at[k - 1], links.along_z(k))
        for k in (2, 1, 3)
    ]
    yield
    for made in copies:
        made.wait_recv()

    def total(kind):
        value = middle[kind, z].astype(jnp.float32)
        for k in range(3):
            value = value + arrived[k, kind].astype(jnp.float32)
        return value

    key, value = total(0), total(1)
    key = key * cosine[...] - pltpu.roll(key, HD // 2, 1) * sines[...]
    keeps_key = lax.rem(y, 2) == 0
    handed[...] = jnp.where(keeps_key, value, key).astype(jnp.bfloat16)
    passed = links.copy(handed, grads.at[y, :, pl.ds(HD, HD)], links.along_y(3))
    grads[y, :, HD:] = jnp.where(keeps_key, key, value).astype(jnp.bfloat16)
    yield
    passed.wait_recv()


def sum_kv_scratch(rows):
    def vmem(*dims):
        return pltpu.VMEM(dims + (rows, HD), jnp.bfloat16)

    return ((vmem(2, 1, 4), vmem(2, 1, 4), vmem(2, 1, 4)), vmem(2, 4), vmem(3, 2), vmem())


def back_kernel(
    heads_out, query_grad, kv_terms, cosine, sines, all_normed, all_d_out, full_q, full_kv, full_out,
    attn_out, d_normed, d_w_qkv, d_w_out,
    scratch, loaded, heads, grads, send, recv, local,
):
    links = Links(send, recv)
    y = links.y
    normed, d_out, w_qkv, w_out = loaded
    loads = [
        local_copy(source, target, local.at[i])
        for i, (source, target) in enumerate(
            [
                (full_out, w_out),
                (all_d_out, d_out),
                (all_normed, normed),
                (full_q, w_qkv.at[:, pl.ds(0, HD)]),
                (full_kv, w_qkv.at[:, pl.ds(HD, HD)]),
            ]
        )
    ]
    for k in (2, 3):
        grads[lax.rem(y + k, SIDE), :, HD:] = jnp.zeros_like(grads[0, :, HD:])
    links.greet(sides=True)

    kv_stream = sum_kv(links, kv_terms, cosine, sines, grads, scratch[0])
    next(kv_stream)
    head_copies, head_mine = exchange_heads(links, heads_out, heads.at[y], local.at[5])
    grad_copies, grad_mine = exchange_heads(
        links, query_grad, grads.at[y, :, pl.ds(0, HD)], local.at[6]
    )

    def keys_part():
        yield from kv_stream
        yield from sum_weight(links, normed, grads.at[:, :, pl.ds(HD, HD)], scratch[5])

    def queries_part():
        for made in grad_copies:
            made.wait_recv()
        grad_mine.wait()
        for made in loads[2:]:
            made.wait()
        yield from sum_weight(links, normed, grads.at[:, :, pl.ds(0, HD)], scratch[4])

    for made in head_copies:
        made.wait_recv()
    head_mine.wait()
    loads[0].wait()
    loads[1].wait()
    streams = {
        "a": sum_groups(links, heads, w_out, attn_out, scratch[1]),
        "k": keys_part(),
        "o": sum_weight(links, d_out, heads, scratch[3]),
        "q": queries_part(),
        "n": sum_groups(links, grads, w_qkv, d_normed, scratch[2]),
    }
    in_order(streams, "akokaqkoknaqnokaqnkonaqknoan")
    links.finish()
    placed_out, placed_q, placed_kv = scratch[3][5], scratch[4][5], scratch[5][5]
    width = SIDE * HD
    for j in range(SIDE):
        d_w_out[:, j * HD : (j + 1) * HD] = placed_out[j]
        d_w_qkv[:, j * HD : (j + 1) * HD] = placed_q[j]
    for kind in range(2):
        total = placed_kv[kind].astype(jnp.float32) + placed_kv[kind + 2].astype(jnp.float32)
        d_w_qkv[:, width + kind * HD : width + (kind + 1) * HD] = total.astype(jnp.bfloat16)


def attention_kernel(
    query_pos, key_pos, cosine, sines, queries, head_grads, kv, heads_out, query_grad, kv_grad, totals
):
    score_scale = HD ** (-0.5)
    keys, values = kv[0], kv[1]
    keys_t, values_t = keys.T, values.T
    rows = 256
    totals[...] = jnp.zeros_like(totals)

    def step(i, carry):
        at = pl.ds(pl.multiple_of(i * rows, rows), rows)
        q, grads = queries[at], head_grads[at]
        allowed = key_pos[...] <= query_pos[...]
        scores = (
            lax.dot_general(keys, q, contract_last, preferred_element_type=jnp.float32) * score_scale
        )
        scores = jnp.where(allowed, scores, masked_score)
        row_max = jnp.max(scores, axis=0, keepdims=True)
        raw = jnp.where(allowed, jnp.exp(scores - row_max), 0.0)
        row_sum = jnp.sum(raw, axis=0, keepdims=True)
        weighted = jnp.dot(values_t, raw.astype(jnp.bfloat16), preferred_element_type=jnp.float32)
        out = (weighted / row_sum).astype(jnp.bfloat16).astype(jnp.float32)
        row_dots = jnp.sum(grads.astype(jnp.float32).T * out, axis=0, keepdims=True)
        weights = raw * (1.0 / row_sum)
        dweights = lax.dot_general(values, grads, contract_last, preferred_element_type=jnp.float32)
        dscores = (weights * (dweights - row_dots)).astype(jnp.bfloat16)
        heads_out[at] = out.T.astype(jnp.bfloat16)
        dq = jnp.dot(keys_t, dscores, preferred_element_type=jnp.float32).T * score_scale
        dq = dq * cosine[...] - pltpu.roll(dq, HD // 2, 1) * sines[...]
        query_grad[at] = dq.astype(jnp.bfloat16)
        totals[0] += jnp.dot(dscores, q, preferred_element_type=jnp.float32) * score_scale
        totals[1] += jnp.dot(weights.astype(jnp.bfloat16), grads, preferred_element_type=jnp.float32)
        return carry

    lax.fori_loop(0, queries.shape[0] // rows, step, 0)
    kv_grad[...] = totals[...].astype(jnp.bfloat16)


VMEM = pl.BlockSpec(memory_space=pltpu.VMEM)
HBM = pl.BlockSpec(memory_space=pl.ANY)


def call(kernel, outs, ins, in_specs, out_specs, scratch, identity=None, copies=0, locals_=0, limit=None):
    if copies:
        scratch = list(scratch) + [
            pltpu.SemaphoreType.DMA((copies,)),
            pltpu.SemaphoreType.DMA((copies,)),
            pltpu.SemaphoreType.DMA((locals_,)),
        ]
    return pl.pallas_call(
        kernel,
        out_shape=outs,
        in_specs=in_specs,
        out_specs=out_specs,
        scratch_shapes=scratch,
        compiler_params=pltpu.CompilerParams(
            collective_id=identity,
            has_side_effects=identity is not None,
            vmem_limit_bytes=limit and limit * 2**20,
        ),
    )(*ins)


def shape(*dims):
    return jax.ShapeDtypeStruct(dims, jnp.bfloat16)


def body(normed, w_qkv, w_out, block_order, d_out):
    rows, model = normed.shape[1], normed.shape[2]
    block_rows = rows // 2
    part = w_out.shape[0]
    length = rows * lax.axis_size("ctx")
    y = lax.axis_index("dp")
    query_pos = stored_positions(
        block_order,
        lax.axis_index("ctx") * rows + jnp.arange(rows, dtype=jnp.int32),
        block_rows,
    )
    all_pos = stored_positions(block_order, jnp.arange(length, dtype=jnp.int32), block_rows)
    cosine, sines = rope_tables(query_pos, HD)

    all_normed, all_d_out, full_q, full_kv, full_out = call(
        front_kernel,
        [
            shape(4, rows, model),
            shape(4, rows, model),
            shape(4, 4, 4, part, HD),
            shape(4, 4, 4, part, HD),
            shape(4, 4, 4, part, HD),
        ],
        [normed[0], d_out[0], w_qkv, w_out],
        [HBM] * 4,
        [HBM] * 5,
        [pltpu.VMEM((2, rows, model), jnp.bfloat16)],
        identity=1,
        copies=3 * 10 + 2 * 8,
        locals_=5,
    )
    full_q, full_kv, full_out = (full.reshape(model, HD) for full in (full_q, full_kv, full_out))

    projected = jnp.dot(
        all_normed.reshape(4 * rows, model),
        jnp.concatenate([full_q, full_kv], axis=1),
        preferred_element_type=jnp.float32,
    ).reshape(4, rows, 2 * HD)
    head_grads = (
        jnp.dot(all_d_out.reshape(4 * rows, model), full_out, preferred_element_type=jnp.float32)
        .astype(jnp.bfloat16)
        .reshape(4, rows, HD)
    )
    queries = projected[:, :, :HD]
    queries = (queries * cosine + swap_halves(queries) * sines).astype(jnp.bfloat16)
    kv = jnp.stack(
        [
            lax.dynamic_index_in_dim(projected, lax.rem(y + k, 4), 0, keepdims=False)[:, HD:]
            for k in (0, 1)
        ]
    )
    turned = kv * cosine + swap_halves(kv) * sines
    kv = jnp.where(lax.rem(y, 2) == 0, turned, kv).astype(jnp.bfloat16)
    all_queries, all_grads, all_kv = call(
        middle_kernel,
        [shape(4, rows, HD), shape(4, rows, HD), shape(2, 4, 4, rows, HD)],
        [queries, head_grads, kv],
        [HBM] * 3,
        [HBM] * 3,
        [],
        identity=2,
        copies=1 + 6 + 3 + 4,
        locals_=3,
    )
    heads_out, query_grad, kv_terms = call(
        attention_kernel,
        [shape(4 * rows, HD), shape(4 * rows, HD), shape(2, length, HD)],
        [
            jnp.concatenate([query_pos, query_pos])[None, :],
            all_pos[:, None],
            jnp.concatenate([cosine, cosine]),
            jnp.concatenate([sines, sines]),
            all_queries.reshape(4 * rows, HD),
            all_grads.reshape(4 * rows, HD),
            all_kv.reshape(2, length, HD),
        ],
        [VMEM] * 7,
        [VMEM] * 3,
        [pltpu.VMEM((2, length, HD), jnp.float32)],
        limit=40,
    )
    width = model // 4
    attn_out, d_normed, d_w_qkv, d_w_out = call(
        back_kernel,
        [shape(rows, width), shape(rows, width), shape(*w_qkv.shape), shape(*w_out.shape)],
        [
            heads_out.reshape(4, rows, HD),
            query_grad.reshape(4, rows, HD),
            kv_terms.reshape(2, 4, 4, rows, HD),
            cosine,
            sines,
            all_normed,
            all_d_out,
            full_q,
            full_kv,
            full_out,
        ],
        [HBM, HBM, VMEM, VMEM, VMEM, HBM, HBM, HBM, HBM, HBM],
        [VMEM] * 4,
        [
            (
                sum_kv_scratch(rows),
                sum_groups_scratch(rows, width),
                sum_groups_scratch(rows, width),
                sum_weight_scratch(part),
                sum_weight_scratch(part),
                sum_weight_scratch(part),
            ),
            (
                pltpu.VMEM((4, rows, model), jnp.bfloat16),
                pltpu.VMEM((4, rows, model), jnp.bfloat16),
                pltpu.VMEM((model, 2 * HD), jnp.bfloat16),
                pltpu.VMEM((model, HD), jnp.bfloat16),
            ),
            pltpu.VMEM((4, rows, HD), jnp.bfloat16),
            pltpu.VMEM((4, rows, 2 * HD), jnp.bfloat16),
        ],
        identity=3,
        copies=10 + 6 + 2 * 9 + 3 * 12,
        locals_=7,
        limit=56,
    )
    return attn_out[None], d_normed[None], d_w_qkv, d_w_out


def solution(mesh):
    in_specs = (
        P("dp", "ctx", None),
        P(("dp", "ctx"), "tp"),
        P(("dp", "ctx"), "tp"),
        P(),
        P("dp", "ctx", None),
    )
    out_specs = (
        P("dp", "ctx", "tp"),
        P("dp", "ctx", "tp"),
        P(("dp", "ctx"), "tp"),
        P(("dp", "ctx"), "tp"),
    )
    return jax.shard_map(body, mesh=mesh, in_specs=in_specs, out_specs=out_specs, check_vma=False)
```

time: 254 us -> 193 us (0.76)
  Pallas kernels: 191 us -> 168 us
  matrix products: 25.1 us -> 7.06 us
  local copies, waits for them, and re-layouts: 29.1 us -> 12.2 us
    pallas_call x2 -> x0, Pallas kernels: 93.8 us -> none  [the longest x1 70.2 us: body(): pl.pallas_call(gather_weights_kernel, out_shape=[shape((4, 4, 4, 2, 32, q...]
    pallas_call x3 -> x4, Pallas kernels: 97.5 us -> 168 us  [call(): pl.pallas_call(kernel, out_shape=outs, in_specs=in_specs, out_specs=out_s...]
    dot_general x6 -> x2, matrix products: 25.1 us -> 7.06 us  [the longest x1 4.54 us: body(): jnp.dot(all_d_out.reshape(4 * rows, model), full_out, preferred_element_t...]
    convert_element_type x2 -> x0, local copies, waits for them, and re-layouts: 15.1 us -> none  [the longest x1 8.63 us: body(): qkv_weight_term = lax.dot_general(tokens, qkv_grads, (((0,), (0,)), ((),...]
    unnamed x17 -> x24, local copies, waits for them, and re-layouts: 10.3 us -> 11.7 us
where the time goes in v2:
time: 193 us; the launch traced here: 192 us
  Pallas kernels  168 us (87%)
  local copies, waits for them, and re-layouts  12.2 us (6%)
  matrix products  7.06 us (4%)
  other arithmetic  3.86 us (2%)
    pallas_call x4, Pallas kernels, call(): pl.pallas_call(kernel, out_shape=outs, in_specs=in_specs, out_specs=out_s...  168 us
    unnamed x24, local copies, waits for them, and re-layouts  11.7 us
    dot_general x1, matrix products, body(): jnp.dot(all_d_out.reshape(4 * rows, model), full_out, preferred_element_t...  4.54 us

profile of v2, /device:TPU:64, one launch (start us, length us, event | category | flops | bytes accessed | tf_op | source)
XLA Modules:
  0.0 192.2 jit_solution(18018651404083432577)
XLA Ops:
  0.7 0.7 select_reduce_fusion.1
  1.5 0.8 select_reduce_fusion
  2.2 0.3 fusion.14
  2.6 0.1 pad_maximum_fusion.1
  2.7 0.0 copy-start.7
  2.7 0.0 copy-start.8
  2.7 0.1 maximum_maximum_fusion
  2.8 0.4 copy.10
  3.2 0.1 fusion.3.key_pos
  3.3 47.7 %shard_map.84 = (bf16[4,128,4096]{2,1,0:T(8,128)(2,1)}, bf16[4,128,4096]{2,1,0:T(8,128)(2,1)}, bf16[4,4,4,64,128]{4,3,2,1,0:T(8,128)(2,1)}, bf16[4,4,4,64,128]{4...) custom-call(bf16[128,4096]{1,0:T(8,128)(2,1)} %bitcast.45, bf16[128,4096]{1,0:T(8,128)(2,1)} %bitcast.46, ...), custom_call_target="tpu_custom_call" | custom-call | tf_op jit(solution)/shard_map/pallas_call | solution.py:584
  51.0 0.0 copy-start.6
  51.0 0.0 copy-start.9
  51.0 4.5 %convolution_convert_fusion = bf16[512,128]{1,0:T(8,128)(2,1)} fusion(bf16[512,4096]{1,0:T(8,128)(2,1)} %bitcast.38, bf16[4096,128]{1,0:T(8,128)(2,1)} %bitcast.43), kind=kOutput, calls=%fused_computation.5 | convolution fusion | flops 536936448 | bytes 5373952 | tf_op jit(solution)/shard_map/dot_general | solution.py:641
  55.6 0.0 copy-done.6
  55.6 0.0 copy-done.9
  55.6 2.5 %fusion = f32[4,128,256]{2,1,0:T(8,128)S(1)} fusion(bf16[4,128,4096]{2,1,0:T(8,128)(2,1)S(1)} %copy-done.6, bf16[4096,128]{1,0:T(8,128)(2,1)} %bitcast.41, bf16[4096,128]{1,0:T(8,128)(2,1)S(1)} %bitcast.40), kind=kOutput, calls=%fused_computation.1 | convolution fusion | flops 1077936128 | bytes 6815744 | tf_op jit(solution)/shard_map/dot_general | solution.py:635
  58.2 0.1 fusion.9
  58.3 0.7 fusion.13.kv
  59.0 0.1 fusion.22
  59.1 0.0 copy-done.7
  59.1 0.0 copy-done.8
  59.2 0.8 fusion.8.queries
  60.0 26.1 %shard_map.85 = (bf16[4,128,128]{2,1,0:T(8,128)(2,1)}, bf16[4,128,128]{2,1,0:T(8,128)(2,1)}, bf16[2,4,4,128,128]{4,3,2,1,0:T(8,128)(2,1)}) custom-call(bf16[4,128,128]{2,1,0:T(8,128)(2,1)} %fusion.8.queries, bf16[4,128,128]{2,1,0:T(8,128)(2,1)} %bitcast.49, bf16[2,128,128]{2,1,0:T(8,128)(2,1)} %fusion.13.kv), custom_call_target="tpu_custom_call" | custom-call | tf_op jit(solution)/shard_map/pallas_call | solution.py:584
  86.1 0.0 copy-start.1
  86.1 1.2 copy-done.1
  87.3 0.0 copy-start.4
  87.3 0.9 copy-done.4
  88.2 0.0 copy-start.5
  88.2 0.9 copy-done.5
  89.1 6.0 %shard_map.86 = (bf16[512,128]{1,0:T(8,128)(2,1)S(1)}, bf16[512,128]{1,0:T(8,128)(2,1)S(1)}, bf16[2,2048,128]{2,1,0:T(8,128)(2,1)S(1)}) custom-call(s32[1,256]{1,0:T(1,128)S(1)} %bitcast.37, s32[2048,1]{1,0:T(8,128)S(1)} %fusion.3.key_pos, f32[256,128]{1,0:T(8,128)S(1)} %get-tuple-element.45.cosine, f32[256,128]{1,0:T(8,128)S(1)} %get-tuple-element.46.sines, ...), custom_call_target="tpu_custom_call" | custom-call | tf_op jit(solution)/shard_map/pallas_call | solution.py:584
  95.1 0.0 copy-start
  95.1 1.0 copy-done
  96.1 0.0 copy-start.2
  96.1 0.7 copy-done.2
  96.8 0.0 copy-start.3
  96.8 0.7 copy-done.3
  97.4 88.5 %shard_map.87 = (bf16[128,1024]{1,0:T(8,128)(2,1)}, bf16[128,1024]{1,0:T(8,128)(2,1)}, bf16[64,768]{1,0:T(8,128)(2,1)}, bf16[64,512]{1,0:T(8,128)(2,1)}) custom-call(bf16[4,128,128]{2,1,0:T(8,128)(2,1)} %bitcast.33, bf16[4,128,128]{2,1,0:T(8,128)(2,1)} %bitcast.34, bf16[2,4,4,128,128]{4,3,2,1,0:T(8,128)(2,1)} %bitcast.31, f32[128,128]{1,0:T(8,128)} %copy-done.7, ...), custom_call_target="tpu_custom_call" | custom-call | tf_op jit(solution)/shard_map/pallas_call | solution.py:584
  185.9 1.7 copy.15
  187.6 1.7 copy.16
  189.2 1.5 copy.17
  190.8 1.5 copy.18
  (8 shorter events, 0.1 us)
Async XLA Ops:
  2.7 56.5 %copy-start.7 = (f32[128,128]{1,0:T(8,128)}, f32[128,128]{1,0:T(8,128)S(1)}, u32[]{:S(2)}) copy-start(f32[128,128]{1,0:T(8,128)S(1)} %get-tuple-element.47.cosine) | copy-start | bytes 196612
  2.7 56.5 %copy-start.8 = (f32[128,128]{1,0:T(8,128)}, f32[128,128]{1,0:T(8,128)S(1)}, u32[]{:S(2)}) copy-start(f32[128,128]{1,0:T(8,128)S(1)} %get-tuple-element.48.sines) | copy-start | bytes 196612
  51.0 4.6 %copy-start.6 = (bf16[4,128,4096]{2,1,0:T(8,128)(2,1)S(1)}, bf16[4,128,4096]{2,1,0:T(8,128)(2,1)}, u32[]{:S(2)}) copy-start(bf16[4,128,4096]{2,1,0:T(8,128)(2,1)} %get-tuple-element.19.all_normed) | copy-start | bytes 12582916
  51.0 4.6 %copy-start.9 = (bf16[4,4,4,64,128]{4,3,2,1,0:T(8,128)(2,1)S(1)}, bf16[4,4,4,64,128]{4,3,2,1,0:T(8,128)(2,1)}, u32[]{:S(2)}) copy-start(bf16[4,4,4,64,128]{4,3,2,1,0:T(8,128)(2,1)} %get-tuple-element.20) | copy-start | bytes 3145732
  86.1 1.2 copy-start.1
  87.3 0.9 copy-start.4
  88.2 0.9 copy-start.5
  95.1 1.0 copy-start
  96.1 0.7 copy-start.2
  96.8 0.7 copy-start.3

commit v3 on v2

v3 whole, which is shorter than its diff:
```python
import jax
import jax.numpy as jnp
from jax import lax
from jax.experimental import pallas as pl
from jax.experimental.pallas import tpu as pltpu
from jax.sharding import PartitionSpec as P

HD = 128
SIDE = 4
MESH = pl.DeviceIdType.MESH

rope_base = 500000.0
masked_score = -1e30
contract_last = (((1,), (1,)), ((), ()))
contract_first = (((0,), (0,)), ((), ()))


def stored_positions(order, row_ids, block_rows):
    owner = row_ids // block_rows
    matches = owner[:, None] == jnp.arange(order.shape[0], dtype=jnp.int32)[None, :]
    picked = jnp.sum(jnp.where(matches, order[None, :], 0), axis=1)
    return picked * block_rows + row_ids % block_rows


def rope_tables(positions, head_size):
    half_size = head_size // 2
    frequency = rope_base ** (-2.0 * jnp.arange(half_size, dtype=jnp.float32) / head_size)
    angles = positions.astype(jnp.float32)[:, None] * frequency[None, :]
    sines = jnp.sin(angles)
    cosine = jnp.cos(angles)
    return (
        jnp.concatenate([cosine, cosine], axis=1),
        jnp.concatenate([-sines, sines], axis=1),
    )


class Links:
    def __init__(self, send, recv):
        self.send, self.recv, self.used, self.copies = send, recv, 0, []
        self.y = lax.axis_index("dp")
        self.c = lax.axis_index("ctx")
        self.t = lax.axis_index("tp")
        self.x = self.c // SIDE
        self.z = self.c % SIDE
        self.core = lax.rem(self.t, 2)
        self.side = self.t // 2

    def along_y(self, k):
        return (lax.rem(self.y + k, SIDE), self.c, self.t)

    def along_x(self, k):
        return (self.y, lax.rem(self.x + k, SIDE) * SIDE + self.z, self.t)

    def along_z(self, k):
        return (self.y, self.x * SIDE + lax.rem(self.z + k, SIDE), self.t)

    def other_core(self):
        return (self.y, self.c, self.t + 1 - 2 * self.core)

    def other_side(self):
        return (self.y, self.c, lax.rem(self.t + 2, 4))

    def greet(self):
        partners = (
            [self.along_y(k) for k in (1, 2, 3)]
            + [self.along_z(k) for k in (1, 2, 3)]
            + [self.along_x(1), self.along_x(3), self.other_core(), self.other_side()]
        )
        barrier = pltpu.get_barrier_semaphore()
        for partner in partners:
            pl.semaphore_signal(barrier, inc=1, device_id=partner, device_id_type=MESH)
        pl.semaphore_wait(barrier, len(partners))

    def copy(self, source, target, partner):
        made = pltpu.make_async_remote_copy(
            src_ref=source,
            dst_ref=target,
            send_sem=self.send.at[self.used],
            recv_sem=self.recv.at[self.used],
            device_id=partner,
            device_id_type=MESH,
        )
        made.start()
        self.used += 1
        self.copies.append(made)
        return made

    def finish(self):
        for made in self.copies:
            made.wait_send()


def local_copy(source, target, semaphore):
    made = pltpu.make_async_copy(source, target, semaphore)
    made.start()
    return made


def in_order(streams, order):
    for name in order:
        next(streams[name], None)


def to_end(streams):
    for stream in streams.values():
        for _ in stream:
            pass


def column(i, width=HD):
    return pl.ds(pl.multiple_of(i * width, width), width)


def ring_gather(links, along, here, view, arrived=None):
    before, after, across = (
        lax.rem(here + 3, SIDE),
        lax.rem(here + 1, SIDE),
        lax.rem(here + 2, SIDE),
    )
    arrived = arrived or (lambda block: None)
    own = view(here, None)
    right = links.copy(own, own, along(1))
    left = links.copy(own, own, along(3))
    yield
    right.wait_recv()
    passed = view(before, 0)
    onward = links.copy(passed, passed, along(1))
    left.wait_recv()
    passed = view(after, 1)
    back = links.copy(passed, passed, along(3))
    arrived(view(before, None))
    arrived(view(after, None))
    yield
    onward.wait_recv()
    arrived(view(across, 0))
    back.wait_recv()
    arrived(view(across, 1))


def gather_columns(links, source, chosen, full):
    y, x, z = links.y, links.x, links.z
    place = full.at[y, x, z]
    copies = [
        links.copy(source.at[:, column(chosen(lax.rem(y + k, SIDE)))], place, links.along_y(k))
        for k in (2, 1, 3)
    ]
    yield
    for made in copies:
        made.wait_recv()
    block = full.at[:, x, z]
    copies = [links.copy(block, block, links.along_z(k)) for k in (2, 1, 3)]
    yield
    for made in copies:
        made.wait_recv()
    yield from ring_gather(
        links,
        links.along_x,
        x,
        lambda i, h: full.at[:, i] if h is None else full.at[pl.ds(2 * h, 2), i],
    )


def gather_tokens(links, full):
    half = full.shape[1] // 2
    first = pl.multiple_of(links.core * half, half)
    handed = []

    def view(i, h):
        if h is None:
            return full.at[i, pl.ds(first, half)]
        return full.at[i, pl.ds(pl.multiple_of(first + h * (half // 2), half // 2), half // 2)]

    def hand(block):
        handed.append(links.copy(block, block, links.other_core()))

    yield from ring_gather(links, links.along_y, links.y, view, hand)
    yield
    for made in handed:
        made.wait_recv()


def gather_kind(links, full):
    x, z = links.x, links.z
    block = full.at[x, z]
    copies = [links.copy(block, block, links.along_z(k)) for k in (2, 1, 3)]
    yield
    for made in copies:
        made.wait_recv()
    yield from ring_gather(
        links,
        links.along_x,
        x,
        lambda i, h: full.at[i] if h is None else full.at[i, pl.ds(2 * h, 2)],
    )


def exchange_heads(links, source, place, own_semaphore):
    copies = [
        links.copy(source.at[lax.rem(links.y + k, SIDE)], place, links.along_y(k))
        for k in (2, 1, 3)
    ]
    return copies, local_copy(source.at[links.y], place, own_semaphore)


def add_blocks(target, *terms):
    lead, (height, width) = target.shape[:-2], target.shape[-2:]
    rows = min(height, max(16, 16384 // width))
    per = height // rows
    count = per
    for size in lead:
        count *= size

    def step(i, carry):
        at = (pl.ds(pl.multiple_of(i % per * rows, rows), rows),)
        rest = i // per
        for size in lead[::-1]:
            at = (rest % size,) + at
            rest = rest // size
        total = terms[0][at].astype(jnp.float32)
        for term in terms[1:]:
            total = total + term[at].astype(jnp.float32)
        target[at] = total.astype(target.dtype)
        return carry

    lax.fori_loop(0, count, step, 0)


def ring_sum(links, along, here, view, result, scratch, prepare=None):
    passing, from_left, from_right = scratch
    left, right, across = (
        lax.rem(here + 3, SIDE),
        lax.rem(here + 1, SIDE),
        lax.rem(here + 2, SIDE),
    )
    prepare = prepare or (lambda i: None)
    prepare(across)
    first = links.copy(view(across, 0), passing.at[0], along(1))
    second = links.copy(view(across, 1), passing.at[1], along(3))
    prepare(right)
    plain_right = links.copy(view(right, 1), from_left.at[1], along(1))
    prepare(left)
    plain_left = links.copy(view(left, 0), from_right.at[0], along(3))
    yield
    prepare(here)
    first.wait_recv()
    add_blocks(passing.at[0], passing.at[0], view(right, 0))
    summed_right = links.copy(passing.at[0], from_left.at[0], along(1))
    second.wait_recv()
    add_blocks(passing.at[1], passing.at[1], view(left, 1))
    summed_left = links.copy(passing.at[1], from_right.at[1], along(3))
    yield
    plain_left.wait_recv()
    summed_right.wait_recv()
    add_blocks(result(0), view(here, 0), from_left.at[0], from_right.at[0])
    plain_right.wait_recv()
    summed_left.wait_recv()
    add_blocks(result(1), view(here, 1), from_left.at[1], from_right.at[1])


def sum_weight(links, tokens, grads, scratch):
    terms, ring, middle, arrived, summed, placed = scratch
    y, x, z = links.y, links.x, links.z
    size = 4 * terms.shape[3]

    def prepare(i):
        def step(owner, carry):
            at = column(owner * SIDE + i, size)
            rows = tokens[:, :, at].reshape(-1, size)
            part = lax.dot_general(
                rows,
                grads[...].reshape(rows.shape[0], HD),
                contract_first,
                preferred_element_type=jnp.float32,
            )
            terms[owner, i] = part.astype(jnp.bfloat16).reshape(terms.shape[2:])
            return carry

        lax.fori_loop(0, SIDE, step, 0)

    yield from ring_sum(
        links,
        links.along_x,
        x,
        lambda i, h: terms.at[pl.ds(2 * h, 2), i],
        lambda h: middle.at[pl.ds(2 * h, 2)],
        ring,
        prepare,
    )
    copies = [
        links.copy(middle.at[:, lax.rem(z + k, SIDE)], arrived.at[k - 1], links.along_z(k))
        for k in (2, 1, 3)
    ]
    yield
    for made in copies:
        made.wait_recv()
    add_blocks(summed, middle.at[:, z], arrived.at[0], arrived.at[1], arrived.at[2])
    copies = [
        links.copy(summed.at[lax.rem(y + k, SIDE)], placed.at[y], links.along_y(k))
        for k in (2, 1, 3)
    ]
    placed[y] = summed[y]
    yield
    for made in copies:
        made.wait_recv()


def sum_weight_scratch(rows):
    def vmem(*dims):
        return pltpu.VMEM(dims + (rows, HD), jnp.bfloat16)

    ring = (vmem(2, 2, 4), vmem(2, 2, 4), vmem(2, 2, 4))
    return (vmem(4, 4, 4), ring, vmem(4, 4), vmem(3, 4), vmem(4), vmem(4))


def sum_groups(links, rows, weights, result, start, scratch):
    terms, near, ring, paired, far = scratch
    whole, width = result.shape[1], terms.shape[3]
    core, side = links.core, links.side
    size = 256

    def prepare(owner):
        def step(i, carry):
            at = owner * (whole // size) + start // size + i
            part = lax.dot_general(
                rows[...].reshape(-1, rows.shape[2]),
                model_rows(weights, at, size),
                contract_last,
                preferred_element_type=jnp.float32,
            )
            terms[owner, :, :, column(i, size)] = part.astype(jnp.bfloat16).reshape(
                SIDE, rows.shape[1], size
            )
            return carry

        lax.fori_loop(0, width // size, step, 0)

    handed = []
    for i in range(2):
        prepare(2 * i + 1 - core)
        handed.append(links.copy(terms.at[2 * i + 1 - core], near.at[i], links.other_core()))
    for i in range(2):
        prepare(2 * i + core)
    yield
    for i in range(2):
        handed[i].wait_recv()
        add_blocks(terms.at[2 * i + core], terms.at[2 * i + core], near.at[i])
    yield from ring_sum(
        links,
        links.along_y,
        links.y,
        lambda i, h: terms.at[2 * h + core, i],
        lambda h: paired.at[h],
        ring,
    )
    across = links.copy(paired.at[1 - side], far, links.other_side())
    yield
    across.wait_recv()
    add_blocks(result.at[:, pl.ds(start, width)], paired.at[side], far)


def sum_groups_scratch(rows, width):
    def vmem(*dims):
        return pltpu.VMEM(dims + (rows, width), jnp.bfloat16)

    return (vmem(4, 4), vmem(2, 4), (vmem(2), vmem(2), vmem(2)), vmem(2), vmem())


def model_rows(weights, i, size):
    parts = [weight[i // 4, i % 4].reshape(size, weight.shape[4]) for weight in weights]
    return parts[0] if len(parts) == 1 else jnp.concatenate(parts, axis=1)


def sum_kind(links, terms, scratch):
    ring, middle, arrived, total = scratch
    x, z = links.x, links.z
    yield from ring_sum(
        links,
        links.along_x,
        x,
        lambda i, h: terms.at[i, pl.ds(2 * h, 2)],
        lambda h: middle.at[pl.ds(2 * h, 2)],
        ring,
    )
    copies = [
        links.copy(middle.at[lax.rem(z + k, SIDE)], arrived.at[k - 1], links.along_z(k))
        for k in (2, 1, 3)
    ]
    yield
    for made in copies:
        made.wait_recv()
    add_blocks(total, middle.at[z], arrived.at[0], arrived.at[1], arrived.at[2])


def sum_kind_scratch(rows):
    def vmem(*dims):
        return pltpu.VMEM(dims + (rows, HD), jnp.bfloat16)

    return ((vmem(2, 2), vmem(2, 2), vmem(2, 2)), vmem(4), vmem(3), pltpu.VMEM((rows, HD), jnp.float32))


def hand_kv(links, key_total, value_total, cosine, sines, grads, handed):
    y = links.y
    key, value = key_total[...], value_total[...]
    key = key * cosine[...] - pltpu.roll(key, HD // 2, 1) * sines[...]
    keeps_key = lax.rem(y, 2) == 0
    handed[...] = jnp.where(keeps_key, value, key).astype(jnp.bfloat16)
    passed = links.copy(handed, grads.at[y, :, pl.ds(HD, HD)], links.along_y(3))
    grads[y, :, HD:] = jnp.where(keeps_key, key, value).astype(jnp.bfloat16)
    yield
    passed.wait_recv()


def project(tokens, weight, target):
    size = 1024

    def step(i, carry):
        rows = tokens[:, :, column(i, size)]
        part = jnp.dot(
            rows.reshape(-1, size),
            weight[i].reshape(size, HD),
            preferred_element_type=jnp.float32,
        ).reshape(target.shape)
        target[...] = jnp.where(i == 0, part, target[...] + part)
        return carry

    lax.fori_loop(0, SIDE, step, 0)


def attend(query_pos, key_pos, cosine, sines, queries, head_grads, kv, heads_out, query_grad, totals):
    score_scale = HD ** (-0.5)
    length = key_pos.shape[0]
    pair = 2
    rows = pair * queries.shape[1]
    keys, values = kv[0].reshape(length, HD), kv[1].reshape(length, HD)
    keys_t, values_t = keys.T, values.T
    turn = jnp.concatenate([cosine[...]] * pair), jnp.concatenate([sines[...]] * pair)
    totals[...] = jnp.zeros_like(totals)

    def step(i, carry):
        at = pl.ds(i * pair, pair)
        q, grads = queries[at].reshape(rows, HD), head_grads[at].reshape(rows, HD)
        allowed = key_pos[...] <= query_pos[...]
        scores = (
            lax.dot_general(keys, q, contract_last, preferred_element_type=jnp.float32) * score_scale
        )
        scores = jnp.where(allowed, scores, masked_score)
        row_max = jnp.max(scores, axis=0, keepdims=True)
        raw = jnp.where(allowed, jnp.exp(scores - row_max), 0.0)
        row_sum = jnp.sum(raw, axis=0, keepdims=True)
        weighted = jnp.dot(values_t, raw.astype(jnp.bfloat16), preferred_element_type=jnp.float32)
        out = (weighted / row_sum).astype(jnp.bfloat16).astype(jnp.float32)
        row_dots = jnp.sum(grads.astype(jnp.float32).T * out, axis=0, keepdims=True)
        weights = raw * (1.0 / row_sum)
        dweights = lax.dot_general(values, grads, contract_last, preferred_element_type=jnp.float32)
        dscores = (weights * (dweights - row_dots)).astype(jnp.bfloat16)
        heads_out[at] = out.T.astype(jnp.bfloat16).reshape(pair, -1, HD)
        dq = jnp.dot(keys_t, dscores, preferred_element_type=jnp.float32).T * score_scale
        dq = dq * turn[0] - pltpu.roll(dq, HD // 2, 1) * turn[1]
        query_grad[at] = dq.astype(jnp.bfloat16).reshape(pair, -1, HD)
        totals[0] += jnp.dot(dscores, q, preferred_element_type=jnp.float32) * score_scale
        totals[1] += jnp.dot(weights.astype(jnp.bfloat16), grads, preferred_element_type=jnp.float32)
        return carry

    lax.fori_loop(0, queries.shape[0] // pair, step, 0)


def whole_kernel(
    normed, d_out, w_qkv, w_out, query_pos, key_pos, cosine, sines,
    attn_out, d_normed, d_w_qkv, d_w_out,
    tokens, weights, blocks, wide, rows_kv, sums, send, recv, local,
):
    links = Links(send, recv)
    y, x, z = links.y, links.x, links.z
    heads = w_out.shape[1] // HD
    all_normed, all_d_out = tokens
    full_q, full_kv, full_out = weights
    my_queries, my_grads, queries, head_grads, heads_out, query_grad, all_heads = blocks
    projected, grads = wide
    my_kv, all_kv, totals, kv_terms, handed = rows_kv
    after = lax.rem(y + 1, SIDE)

    given = {
        "q": (w_qkv, lambda j: j, full_q),
        "k": (w_qkv, lambda j: heads + lax.rem(j, 2), full_kv),
        "o": (w_out, lambda j: j, full_out),
    }
    mine = [
        local_copy(source.at[:, column(chosen(y))], full.at[y, x, z], local.at[i])
        for i, (source, chosen, full) in enumerate(given.values())
    ]
    mine += [
        local_copy(source.at[0], full.at[y], local.at[3 + i])
        for i, (source, full) in enumerate(((normed, all_normed), (d_out, all_d_out)))
    ]
    for k in (2, 3):
        grads[lax.rem(y + k, SIDE), :, HD:] = jnp.zeros_like(grads[0, :, HD:])
    links.greet()
    streams = {name: gather_columns(links, *parts) for name, parts in given.items()}
    streams["n"] = gather_tokens(links, all_normed)
    streams["d"] = gather_tokens(links, all_d_out)
    for made in mine:
        made.wait()
    in_order(streams, "qknoqkoqndkqkoqnknnqk")

    project(all_normed.at[pl.ds(0, SIDE)], full_kv, projected)
    for i, sequence in enumerate((y, after)):
        part = projected[sequence]
        turned = part * cosine[...] + pltpu.roll(part, HD // 2, 1) * sines[...]
        my_kv[i] = jnp.where(lax.rem(y, 2) == 0, turned, part).astype(jnp.bfloat16)
    place = all_kv.at[lax.rem(y, 2), x, z]
    passed = links.copy(my_kv.at[1], place, links.along_y(1))
    place[...] = my_kv[0]
    project(all_normed, full_q, projected)
    for i in range(SIDE):
        part = projected[i]
        turned = part * cosine[...] + pltpu.roll(part, HD // 2, 1) * sines[...]
        my_queries[i] = turned.astype(jnp.bfloat16)
    passed.wait_recv()
    streams["K"] = gather_kind(links, all_kv.at[0])
    streams["V"] = gather_kind(links, all_kv.at[1])
    in_order(streams, "KV")
    query_copies, query_mine = exchange_heads(links, my_queries, queries.at[y], local.at[0])
    in_order(streams, "odKVoddooddd")
    project(all_d_out, full_out, projected)
    my_grads[...] = projected[...].astype(jnp.bfloat16)
    grad_copies, grad_mine = exchange_heads(links, my_grads, head_grads.at[y], local.at[1])
    in_order(streams, "KVKV")
    to_end(streams)
    for made in query_copies + grad_copies:
        made.wait_recv()
    query_mine.wait()
    grad_mine.wait()

    attend(query_pos, key_pos, cosine, sines, queries, head_grads, all_kv, heads_out, query_grad, totals)
    kv_terms[...] = totals[...].astype(jnp.bfloat16).reshape(kv_terms.shape)

    streams = {
        "K": sum_kind(links, kv_terms.at[0], sums[0]),
        "V": sum_kind(links, kv_terms.at[1], sums[1]),
    }
    in_order(streams, "KV")
    head_copies, head_mine = exchange_heads(links, heads_out, all_heads.at[y], local.at[0])
    grad_copies, grad_mine = exchange_heads(
        links, query_grad, grads.at[y, :, pl.ds(0, HD)], local.at[1]
    )
    for made in head_copies:
        made.wait_recv()
    head_mine.wait()
    half = sums[2][0].shape[3]
    qkv = (full_q, full_kv)
    streams["a"] = sum_groups(links, all_heads, (full_out,), attn_out, 0, sums[2])
    streams["b"] = sum_groups(links, all_heads, (full_out,), attn_out, half, sums[3])
    streams["o"] = sum_weight(links, all_d_out, all_heads, sums[6])
    streams["q"] = sum_weight(links, all_normed, grads.at[:, :, pl.ds(0, HD)], sums[7])
    in_order(streams, "aKVbaKoVK")
    for made in grad_copies:
        made.wait_recv()
    grad_mine.wait()
    in_order(streams, "qV")
    streams["h"] = hand_kv(links, sums[0][3], sums[1][3], cosine, sines, grads, handed)
    in_order(streams, "hbaoh")
    streams["n"] = sum_groups(links, grads, qkv, d_normed, 0, sums[4])
    streams["m"] = sum_groups(links, grads, qkv, d_normed, half, sums[5])
    streams["w"] = sum_weight(links, all_normed, grads.at[:, :, pl.ds(HD, HD)], sums[8])
    in_order(streams, "nqmbnwmaoqbwnmaoqwbnmoqwnmw")
    to_end(streams)
    links.finish()
    placed_out, placed_q, placed_kv = sums[6][5], sums[7][5], sums[8][5]
    width = SIDE * HD
    for j in range(SIDE):
        d_w_out[:, j * HD : (j + 1) * HD] = placed_out[j]
        d_w_qkv[:, j * HD : (j + 1) * HD] = placed_q[j]
    for kind in range(2):
        total = placed_kv[kind].astype(jnp.float32) + placed_kv[kind + 2].astype(jnp.float32)
        d_w_qkv[:, width + kind * HD : width + (kind + 1) * HD] = total.astype(jnp.bfloat16)


def hand_on_kernel(*refs):
    half = len(refs) // 2
    for source, target in zip(refs[:half], refs[half:]):
        target[...] = source[...].reshape(target.shape)


VMEM = pl.BlockSpec(memory_space=pltpu.VMEM)
HBM = pl.BlockSpec(memory_space=pl.ANY)


def shape(*dims):
    return jax.ShapeDtypeStruct(dims, jnp.bfloat16)


def body(normed, w_qkv, w_out, block_order, d_out):
    rows, model = normed.shape[1], normed.shape[2]
    block_rows = rows // 2
    part = w_out.shape[0]
    length = rows * lax.axis_size("ctx")
    query_pos = stored_positions(
        block_order,
        lax.axis_index("ctx") * rows + jnp.arange(rows, dtype=jnp.int32),
        block_rows,
    )
    all_pos = stored_positions(block_order, jnp.arange(length, dtype=jnp.int32), block_rows)
    cosine, sines = rope_tables(query_pos, HD)
    width = model // 4

    def vmem(*dims, kind=jnp.bfloat16):
        return pltpu.VMEM(dims, kind)

    blocks = vmem(4, rows, HD)
    copies = 5 * 8 + 2 * 3 + 1 + 2 * 7 + 4 * 3 + 2 * 9 + 1 + 4 * 9 + 3 * 12
    outs = [shape(rows, width), shape(rows, width), shape(*w_qkv.shape), shape(*w_out.shape)]
    results = pl.pallas_call(
        whole_kernel,
        out_shape=outs,
        in_specs=[HBM] * 4 + [VMEM] * 4,
        out_specs=[VMEM] * 4,
        scratch_shapes=[
            (vmem(4, rows, model),) * 2,
            (vmem(4, 4, 4, part, HD),) * 3,
            (blocks,) * 7,
            (vmem(4, rows, HD, kind=jnp.float32), vmem(4, rows, 2 * HD)),
            (
                vmem(2, rows, HD),
                vmem(2, 4, 4, rows, HD),
                vmem(2, length, HD, kind=jnp.float32),
                vmem(2, 4, 4, rows, HD),
                vmem(rows, HD),
            ),
            (sum_kind_scratch(rows),) * 2
            + (sum_groups_scratch(rows, width // 2),) * 4
            + (sum_weight_scratch(part),) * 3,
            pltpu.SemaphoreType.DMA((copies,)),
            pltpu.SemaphoreType.DMA((copies,)),
            pltpu.SemaphoreType.DMA((5,)),
        ],
        compiler_params=pltpu.CompilerParams(
            collective_id=1, has_side_effects=True, vmem_limit_bytes=60 * 2**20
        ),
    )(
        normed,
        d_out,
        w_qkv,
        w_out,
        jnp.concatenate([query_pos, query_pos])[None, :],
        all_pos[:, None],
        cosine,
        sines,
    )
    outs = [shape(1, rows, width)] * 2 + outs[2:]
    return pl.pallas_call(hand_on_kernel, out_shape=outs)(*results)


def solution(mesh):
    in_specs = (
        P("dp", "ctx", None),
        P(("dp", "ctx"), "tp"),
        P(("dp", "ctx"), "tp"),
        P(),
        P("dp", "ctx", None),
    )
    out_specs = (
        P("dp", "ctx", "tp"),
        P("dp", "ctx", "tp"),
        P(("dp", "ctx"), "tp"),
        P(("dp", "ctx"), "tp"),
    )
    return jax.shard_map(body, mesh=mesh, in_specs=in_specs, out_specs=out_specs, check_vma=False)
```

time: 193 us -> 160 us (0.83)
  Pallas kernels: 168 us -> 154 us
  local copies, waits for them, and re-layouts: 12.2 us -> 0.99 us
  matrix products: 7.06 us -> 0 us
    pallas_call x4 -> x2, Pallas kernels: 168 us -> 154 us  [the longest x1 152 us: body(): pl.pallas_call(whole_kernel, out_shape=outs, in_specs=[HBM] * 4 + [VMEM]...]
    unnamed x24 -> x2, local copies, waits for them, and re-layouts: 11.7 us -> 0.63 us
    dot_general x2 -> x0, matrix products: 7.06 us -> none  [the longest x1 4.54 us: body(): jnp.dot(all_d_out.reshape(4 * rows, model), full_out, preferred_element_t...]
where the time goes in v3:
time: 160 us; the launch traced here: 159 us
  Pallas kernels  154 us (96%)
  other arithmetic  2.99 us (2%)
    pallas_call x1, Pallas kernels, body(): pl.pallas_call(whole_kernel, out_shape=outs, in_specs=[HBM] * 4 + [VMEM]...  152 us

profile of v3, /device:TPU:64, one launch (start us, length us, event | category | flops | bytes accessed | tf_op | source)
XLA Modules:
  0.0 158.9 jit_solution(6154088673955733486)
XLA Ops:
  0.6 0.0 copy-start
  0.7 0.6 copy-done
  1.3 0.1 select_reduce_fusion.1
  1.4 0.6 pad_add_fusion
  2.0 0.1 select_reduce_fusion
  2.1 0.3 fusion.4
  2.4 0.8 pad_maximum_fusion
  3.2 0.4 copy.10
  3.6 1.1 fusion.key_pos
  4.7 152.3 %shard_map.84 = (bf16[128,1024]{1,0:T(8,128)(2,1)}, bf16[128,1024]{1,0:T(8,128)(2,1)}, bf16[64,768]{1,0:T(8,128)(2,1)}, bf16[64,512]{1,0:T(8,128)(2,1)}) custom-call(bf16[1,128,4096]{2,1,0:T(8,128)(2,1)} %normed.1, bf16[1,128,4096]{2,1,0:T(8,128)(2,1)} %d_out.1, bf16[64,768]{1,0:T(8,128)(2,1)} %w_qkv.1, bf16[64,512]{1,0:T(8,128)(2,1)} %w_out.1, ...), custom_call_target="tpu_custom_call" | custom-call | tf_op jit(solution)/shard_map/pallas_call | solution.py:612
  157.0 1.9 %shard_map.85 = (bf16[1,128,1024]{2,1,0:T(8,128)(2,1)}, bf16[1,128,1024]{2,1,0:T(8,128)(2,1)}, bf16[64,768]{1,0:T(8,128)(2,1)}, bf16[64,512]{1,0:T(8,128)(2,1)}) custom-call(bf16[128,1024]{1,0:T(8,128)(2,1)} %get-tuple-element.8.refs_0_, bf16[128,1024]{1,0:T(8,128)(2,1)} %get-tuple-element.9.refs_1_, bf16[64,768]{1,0:T(8,128)(2,1)} %get-tuple-element.10.refs_2_, ...), custom_call_target="tpu_custom_call" | custom-call | tf_op jit(solution)/shard_map/pallas_call | solution.py:650
  (5 shorter events, 0.0 us)
Async XLA Ops:
  0.6 0.7 copy-start

commit v4 on v3

--- a/solution.py
+++ b/solution.py
@@ -1,5 +1,6 @@
 import jax
 import jax.numpy as jnp
+import numpy as np
 from jax import lax
 from jax.experimental import pallas as pl
 from jax.experimental.pallas import tpu as pltpu
@@ -13,25 +14,6 @@
 masked_score = -1e30
 contract_last = (((1,), (1,)), ((), ()))
 contract_first = (((0,), (0,)), ((), ()))
-
-
-def stored_positions(order, row_ids, block_rows):
-    owner = row_ids // block_rows
-    matches = owner[:, None] == jnp.arange(order.shape[0], dtype=jnp.int32)[None, :]
-    picked = jnp.sum(jnp.where(matches, order[None, :], 0), axis=1)
-    return picked * block_rows + row_ids % block_rows
-
-
-def rope_tables(positions, head_size):
-    half_size = head_size // 2
-    frequency = rope_base ** (-2.0 * jnp.arange(half_size, dtype=jnp.float32) / head_size)
-    angles = positions.astype(jnp.float32)[:, None] * frequency[None, :]
-    sines = jnp.sin(angles)
-    cosine = jnp.cos(angles)
-    return (
-        jnp.concatenate([cosine, cosine], axis=1),
-        jnp.concatenate([-sines, sines], axis=1),
-    )
 
 
 class Links:
@@ -225,7 +207,7 @@
     lax.fori_loop(0, count, step, 0)
 
 
-def ring_sum(links, along, here, view, result, scratch, prepare=None):
+def ring_sum(links, along, here, view, result, scratch, prepare=None, extra=None):
     passing, from_left, from_right = scratch
     left, right, across = (
         lax.rem(here + 3, SIDE),
@@ -233,6 +215,7 @@
         lax.rem(here + 2, SIDE),
     )
     prepare = prepare or (lambda i: None)
+    extra = extra or (lambda h: ())
     prepare(across)
     first = links.copy(view(across, 0), passing.at[0], along(1))
     second = links.copy(view(across, 1), passing.at[1], along(3))
@@ -251,10 +234,10 @@
     yield
     plain_left.wait_recv()
     summed_right.wait_recv()
-    add_blocks(result(0), view(here, 0), from_left.at[0], from_right.at[0])
+    add_blocks(result(0), view(here, 0), from_left.at[0], from_right.at[0], *extra(0))
     plain_right.wait_recv()
     summed_left.wait_recv()
-    add_blocks(result(1), view(here, 1), from_left.at[1], from_right.at[1])
+    add_blocks(result(1), view(here, 1), from_left.at[1], from_right.at[1], *extra(1))
 
 
 def sum_weight(links, tokens, grads, scratch):
@@ -312,7 +295,7 @@
     return (vmem(4, 4, 4), ring, vmem(4, 4), vmem(3, 4), vmem(4), vmem(4))
 
 
-def sum_groups(links, rows, weights, result, start, scratch):
+def sum_groups(links, rows, weight, result, start, scratch, own_part=None):
     terms, near, ring, paired, far = scratch
     whole, width = result.shape[1], terms.shape[3]
     core, side = links.core, links.side
@@ -322,8 +305,8 @@
         def step(i, carry):
             at = owner * (whole // size) + start // size + i
             part = lax.dot_general(
-                rows[...].reshape(-1, rows.shape[2]),
-                model_rows(weights, at, size),
+                rows[...].reshape(-1, HD),
+                model_rows(weight, at, size),
                 contract_last,
                 preferred_element_type=jnp.float32,
             )
@@ -351,6 +334,9 @@
         lambda i, h: terms.at[2 * h + core, i],
         lambda h: paired.at[h],
         ring,
+        extra=None
+        if own_part is None
+        else lambda h: (own_part.at[2 * h + core, :, pl.ds(start, width)],),
     )
     across = links.copy(paired.at[1 - side], far, links.other_side())
     yield
@@ -365,9 +351,41 @@
     return (vmem(4, 4), vmem(2, 4), (vmem(2), vmem(2), vmem(2)), vmem(2), vmem())
 
 
-def model_rows(weights, i, size):
-    parts = [weight[i // 4, i % 4].reshape(size, weight.shape[4]) for weight in weights]
-    return parts[0] if len(parts) == 1 else jnp.concatenate(parts, axis=1)
+def model_rows(weight, i, size):
+    return weight[i // 4, i % 4].reshape(size, HD)
+
+
+def own_groups(links, pieces, terms, near):
+    core = links.core
+    width, size = terms.shape[2], 256
+
+    def prepare(owner):
+        def step(i, carry):
+            at = owner * (width // size) + i
+            part = sum(
+                lax.dot_general(
+                    rows[...],
+                    model_rows(weight, at, size),
+                    contract_last,
+                    preferred_element_type=jnp.float32,
+                )
+                for rows, weight in pieces
+            )
+            terms[owner, :, column(i, size)] = part.astype(jnp.bfloat16)
+            return carry
+
+        lax.fori_loop(0, width // size, step, 0)
+
+    handed = []
+    for i in range(2):
+        prepare(2 * i + 1 - core)
+        handed.append(links.copy(terms.at[2 * i + 1 - core], near.at[i], links.other_core()))
+    for i in range(2):
+        prepare(2 * i + core)
+    yield
+    for i in range(2):
+        handed[i].wait_recv()
+        add_blocks(terms.at[2 * i + core], terms.at[2 * i + core], near.at[i])
 
 
 def sum_kind(links, terms, scratch):
@@ -396,6 +414,13 @@
         return pltpu.VMEM(dims + (rows, HD), jnp.bfloat16)
 
     return ((vmem(2, 2), vmem(2, 2), vmem(2, 2)), vmem(4), vmem(3), pltpu.VMEM((rows, HD), jnp.float32))
+
+
+def arrive(exchange):
+    copies, own = exchange
+    for made in copies:
+        made.wait_recv()
+    own.wait()
 
 
 def hand_kv(links, key_total, value_total, cosine, sines, grads, handed):
@@ -464,32 +489,58 @@
     lax.fori_loop(0, queries.shape[0] // pair, step, 0)
 
 
+def place_tables(links, order, frequency, query_pos, key_pos, cosine, sines):
+    rows = cosine.shape[0]
+    block = rows // 2
+    first, second = order[2 * links.c] * block, order[2 * links.c + 1] * block
+
+    def positions(dims, axis):
+        row = lax.rem(lax.broadcasted_iota(jnp.int32, dims, axis), rows)
+        return jnp.where(row < block, first, second - block) + row
+
+    query_pos[...] = positions(query_pos.shape, 1)
+    angles = positions(cosine.shape, 0).astype(jnp.float32) * frequency[...]
+    lane = lax.broadcasted_iota(jnp.int32, sines.shape, 1)
+    sine = jnp.sin(angles)
+    cosine[...] = jnp.cos(angles)
+    sines[...] = jnp.where(lane < HD // 2, -sine, sine)
+    row = lax.broadcasted_iota(jnp.int32, (block, 1), 0)
+    for i in range(key_pos.shape[0] // block):
+        key_pos[i * block : (i + 1) * block] = order[i] * block + row
+
+
+FRONT = "kqnokvqknoqdvkqnknoPdPVqKoQVdKVdoGKVvKV"
+BACK = "KVvbKVbaoKbmVoabKqVahonqmahwbqvewmnemqwnonowamnqw"
+
+
 def whole_kernel(
-    normed, d_out, w_qkv, w_out, query_pos, key_pos, cosine, sines,
+    normed, d_out, w_qkv, w_out, order, frequency,
     attn_out, d_normed, d_w_qkv, d_w_out,
-    tokens, weights, blocks, wide, rows_kv, sums, send, recv, local,
+    tables, tokens, weights, blocks, wide, rows_kv, own, sums, send, recv, local,
 ):
     links = Links(send, recv)
     y, x, z = links.y, links.x, links.z
     heads = w_out.shape[1] // HD
+    query_pos, key_pos, cosine, sines = tables
     all_normed, all_d_out = tokens
-    full_q, full_kv, full_out = weights
+    full_q, full_kv, full_out, full_other = weights
     my_queries, my_grads, queries, head_grads, heads_out, query_grad, all_heads = blocks
     projected, grads = wide
     my_kv, all_kv, totals, kv_terms, handed = rows_kv
     after = lax.rem(y + 1, SIDE)
 
     given = {
+        "k": (w_qkv, lambda j: heads + lax.rem(j, 2), full_kv),
         "q": (w_qkv, lambda j: j, full_q),
-        "k": (w_qkv, lambda j: heads + lax.rem(j, 2), full_kv),
         "o": (w_out, lambda j: j, full_out),
+        "v": (w_qkv, lambda j: heads + lax.rem(j + 1, 2), full_other),
     }
     mine = [
         local_copy(source.at[:, column(chosen(y))], full.at[y, x, z], local.at[i])
         for i, (source, chosen, full) in enumerate(given.values())
     ]
     mine += [
-        local_copy(source.at[0], full.at[y], local.at[3 + i])
+        local_copy(source.at[0], full.at[y], local.at[4 + i])
         for i, (source, full) in enumerate(((normed, all_normed), (d_out, all_d_out)))
     ]
     for k in (2, 3):
@@ -500,69 +551,78 @@
     streams["d"] = gather_tokens(links, all_d_out)
     for made in mine:
         made.wait()
-    in_order(streams, "qknoqkoqndkqkoqnknnqk")
-
-    project(all_normed.at[pl.ds(0, SIDE)], full_kv, projected)
-    for i, sequence in enumerate((y, after)):
-        part = projected[sequence]
-        turned = part * cosine[...] + pltpu.roll(part, HD // 2, 1) * sines[...]
-        my_kv[i] = jnp.where(lax.rem(y, 2) == 0, turned, part).astype(jnp.bfloat16)
-    place = all_kv.at[lax.rem(y, 2), x, z]
-    passed = links.copy(my_kv.at[1], place, links.along_y(1))
-    place[...] = my_kv[0]
-    project(all_normed, full_q, projected)
-    for i in range(SIDE):
-        part = projected[i]
-        turned = part * cosine[...] + pltpu.roll(part, HD // 2, 1) * sines[...]
-        my_queries[i] = turned.astype(jnp.bfloat16)
-    passed.wait_recv()
+    in_order(streams, FRONT[:5])
+    place_tables(links, order, frequency, query_pos, key_pos, cosine, sines)
+    held = {}
+
+    def project_kv():
+        for i, sequence in enumerate((y, after)):
+            project(all_normed.at[pl.ds(sequence, 1)], full_kv, projected.at[pl.ds(0, 1)])
+            part = projected[0]
+            turned = part * cosine[...] + pltpu.roll(part, HD // 2, 1) * sines[...]
+            my_kv[i] = jnp.where(lax.rem(y, 2) == 0, turned, part).astype(jnp.bfloat16)
+        place = all_kv.at[lax.rem(y, 2), x, z]
+        passed = links.copy(my_kv.at[1], place, links.along_y(1))
+        place[...] = my_kv[0]
+        yield
+        passed.wait_recv()
+
+    def project_queries():
+        project(all_normed, full_q, projected)
+        for i in range(SIDE):
+            part = projected[i]
+            turned = part * cosine[...] + pltpu.roll(part, HD // 2, 1) * sines[...]
+            my_queries[i] = turned.astype(jnp.bfloat16)
+        held["Q"] = exchange_heads(links, my_queries, queries.at[y], local.at[0])
+        yield
+
+    def project_grads():
+        project(all_d_out, full_out, projected)
+        my_grads[...] = projected[...].astype(jnp.bfloat16)
+        held["G"] = exchange_heads(links, my_grads, head_grads.at[y], local.at[1])
+        yield
+
+    streams["P"] = project_kv()
+    streams["Q"] = project_queries()
+    streams["G"] = project_grads()
     streams["K"] = gather_kind(links, all_kv.at[0])
     streams["V"] = gather_kind(links, all_kv.at[1])
-    in_order(streams, "KV")
-    query_copies, query_mine = exchange_heads(links, my_queries, queries.at[y], local.at[0])
-    in_order(streams, "odKVoddooddd")
-    project(all_d_out, full_out, projected)
-    my_grads[...] = projected[...].astype(jnp.bfloat16)
-    grad_copies, grad_mine = exchange_heads(links, my_grads, head_grads.at[y], local.at[1])
-    in_order(streams, "KVKV")
-    to_end(streams)
-    for made in query_copies + grad_copies:
-        made.wait_recv()
-    query_mine.wait()
-    grad_mine.wait()
-
+    in_order(streams, FRONT[5:])
+    arrive(held.pop("Q"))
+    arrive(held.pop("G"))
     attend(query_pos, key_pos, cosine, sines, queries, head_grads, all_kv, heads_out, query_grad, totals)
     kv_terms[...] = totals[...].astype(jnp.bfloat16).reshape(kv_terms.shape)
 
+    held["heads"] = exchange_heads(links, heads_out, all_heads.at[y], local.at[0])
+    held["grads"] = exchange_heads(links, query_grad, grads.at[y, :, pl.ds(0, HD)], local.at[1])
+
+    def having(name, stream):
+        if name in held:
+            arrive(held.pop(name))
+        yield from stream
+
+    half = sums[2][0].shape[3]
+    own_terms, own_near = own
+    query_part, kv_part = grads.at[:, :, pl.ds(0, HD)], grads.at[:, :, pl.ds(HD, HD)]
+    own_pieces = [(grads.at[y, :, pl.ds(HD, HD)], full_kv), (handed, full_other)]
     streams = {
+        "v": streams["v"],
         "K": sum_kind(links, kv_terms.at[0], sums[0]),
         "V": sum_kind(links, kv_terms.at[1], sums[1]),
+        "h": hand_kv(links, sums[0][3], sums[1][3], cosine, sines, grads, handed),
+        "e": own_groups(links, own_pieces, own_terms, own_near),
+        "w": sum_weight(links, all_normed, kv_part, sums[8]),
     }
-    in_order(streams, "KV")
-    head_copies, head_mine = exchange_heads(links, heads_out, all_heads.at[y], local.at[0])
-    grad_copies, grad_mine = exchange_heads(
-        links, query_grad, grads.at[y, :, pl.ds(0, HD)], local.at[1]
-    )
-    for made in head_copies:
-        made.wait_recv()
-    head_mine.wait()
-    half = sums[2][0].shape[3]
-    qkv = (full_q, full_kv)
-    streams["a"] = sum_groups(links, all_heads, (full_out,), attn_out, 0, sums[2])
-    streams["b"] = sum_groups(links, all_heads, (full_out,), attn_out, half, sums[3])
-    streams["o"] = sum_weight(links, all_d_out, all_heads, sums[6])
-    streams["q"] = sum_weight(links, all_normed, grads.at[:, :, pl.ds(0, HD)], sums[7])
-    in_order(streams, "aKVbaKoVK")
-    for made in grad_copies:
-        made.wait_recv()
-    grad_mine.wait()
-    in_order(streams, "qV")
-    streams["h"] = hand_kv(links, sums[0][3], sums[1][3], cosine, sines, grads, handed)
-    in_order(streams, "hbaoh")
-    streams["n"] = sum_groups(links, grads, qkv, d_normed, 0, sums[4])
-    streams["m"] = sum_groups(links, grads, qkv, d_normed, half, sums[5])
-    streams["w"] = sum_weight(links, all_normed, grads.at[:, :, pl.ds(HD, HD)], sums[8])
-    in_order(streams, "nqmbnwmaoqbwnmaoqwbnmoqwnmw")
+    for name, needs, stream in (
+        ("a", "heads", sum_groups(links, all_heads, full_out, attn_out, 0, sums[2])),
+        ("b", "heads", sum_groups(links, all_heads, full_out, attn_out, half, sums[3])),
+        ("n", "grads", sum_groups(links, query_part, full_q, d_normed, 0, sums[4], own_terms)),
+        ("m", "grads", sum_groups(links, query_part, full_q, d_normed, half, sums[5], own_terms)),
+        ("o", "heads", sum_weight(links, all_d_out, all_heads, sums[6])),
+        ("q", "grads", sum_weight(links, all_normed, query_part, sums[7])),
+    ):
+        streams[name] = having(needs, stream)
+    in_order(streams, BACK)
     to_end(streams)
     links.finish()
     placed_out, placed_q, placed_kv = sums[6][5], sums[7][5], sums[8][5]
@@ -591,32 +651,32 @@
 
 def body(normed, w_qkv, w_out, block_order, d_out):
     rows, model = normed.shape[1], normed.shape[2]
-    block_rows = rows // 2
     part = w_out.shape[0]
     length = rows * lax.axis_size("ctx")
-    query_pos = stored_positions(
-        block_order,
-        lax.axis_index("ctx") * rows + jnp.arange(rows, dtype=jnp.int32),
-        block_rows,
-    )
-    all_pos = stored_positions(block_order, jnp.arange(length, dtype=jnp.int32), block_rows)
-    cosine, sines = rope_tables(query_pos, HD)
+    frequency = rope_base ** (-2.0 * np.arange(HD // 2, dtype=np.float64) / HD)
+    frequency = np.tile(frequency, 2).astype(np.float32)[None, :]
     width = model // 4
 
     def vmem(*dims, kind=jnp.bfloat16):
         return pltpu.VMEM(dims, kind)
 
     blocks = vmem(4, rows, HD)
-    copies = 5 * 8 + 2 * 3 + 1 + 2 * 7 + 4 * 3 + 2 * 9 + 1 + 4 * 9 + 3 * 12
+    copies = 4 * 10 + 2 * 8 + 1 + 2 * 7 + 4 * 3 + 2 * 9 + 1 + 2 + 4 * 9 + 3 * 12
     outs = [shape(rows, width), shape(rows, width), shape(*w_qkv.shape), shape(*w_out.shape)]
     results = pl.pallas_call(
         whole_kernel,
         out_shape=outs,
-        in_specs=[HBM] * 4 + [VMEM] * 4,
+        in_specs=[HBM] * 4 + [pl.BlockSpec(memory_space=pltpu.SMEM), VMEM],
         out_specs=[VMEM] * 4,
         scratch_shapes=[
+            (
+                vmem(1, 2 * rows, kind=jnp.int32),
+                vmem(length, 1, kind=jnp.int32),
+                vmem(rows, HD, kind=jnp.float32),
+                vmem(rows, HD, kind=jnp.float32),
+            ),
             (vmem(4, rows, model),) * 2,
-            (vmem(4, 4, 4, part, HD),) * 3,
+            (vmem(4, 4, 4, part, HD),) * 4,
             (blocks,) * 7,
             (vmem(4, rows, HD, kind=jnp.float32), vmem(4, rows, 2 * HD)),
             (
@@ -626,12 +686,13 @@
                 vmem(2, 4, 4, rows, HD),
                 vmem(rows, HD),
             ),
+            (vmem(4, rows, width), vmem(2, rows, width)),
             (sum_kind_scratch(rows),) * 2
             + (sum_groups_scratch(rows, width // 2),) * 4
             + (sum_weight_scratch(part),) * 3,
             pltpu.SemaphoreType.DMA((copies,)),
             pltpu.SemaphoreType.DMA((copies,)),
-            pltpu.SemaphoreType.DMA((5,)),
+            pltpu.SemaphoreType.DMA((6,)),
         ],
         compiler_params=pltpu.CompilerParams(
             collective_id=1, has_side_effects=True, vmem_limit_bytes=60 * 2**20
@@ -641,10 +702,8 @@
         d_out,
         w_qkv,
         w_out,
-        jnp.concatenate([query_pos, query_pos])[None, :],
-        all_pos[:, None],
-        cosine,
-        sines,
+        block_order,
+        jnp.asarray(frequency),
     )
     outs = [shape(1, rows, width)] * 2 + outs[2:]
     return pl.pallas_call(hand_on_kernel, out_shape=outs)(*results)

time: 160 us -> 140 us (0.88)
  Pallas kernels: 154 us -> 140 us
  other arithmetic: 2.99 us -> 0 us
    pallas_call x1, Pallas kernels: 152 us -> 138 us  [body(): pl.pallas_call(whole_kernel, out_shape=outs, in_specs=[HBM] * 4 + [pl.Blo...]
where the time goes in v4:
time: 140 us
  Pallas kernels  140 us (100%)
    pallas_call x1, Pallas kernels, body(): pl.pallas_call(whole_kernel, out_shape=outs, in_specs=[HBM] * 4 + [pl.Blo...  138 us

profile of v4, /device:TPU:64, one launch (start us, length us, event | category | flops | bytes accessed | tf_op | source)
XLA Modules:
  0.0 140.2 jit_solution(852496616381698187)
XLA Ops:
  0.6 137.6 %shard_map.93 = (bf16[128,1024]{1,0:T(8,128)(2,1)}, bf16[128,1024]{1,0:T(8,128)(2,1)}, bf16[64,768]{1,0:T(8,128)(2,1)}, bf16[64,512]{1,0:T(8,128)(2,1)}) custom-call(bf16[1,128,4096]{2,1,0:T(8,128)(2,1)} %normed.1, bf16[1,128,4096]{2,1,0:T(8,128)(2,1)} %d_out.1, bf16[64,768]{1,0:T(8,128)(2,1)} %w_qkv.1, bf16[64,512]{1,0:T(8,128)(2,1)} %w_out.1, s32[32]{0:T(128)} %order.1, ...), custom_call_target="tpu_custom_call" | custom-call | tf_op jit(solution)/shard_map/pallas_call | solution.py:666
  138.3 1.9 %shard_map.94 = (bf16[1,128,1024]{2,1,0:T(8,128)(2,1)}, bf16[1,128,1024]{2,1,0:T(8,128)(2,1)}, bf16[64,768]{1,0:T(8,128)(2,1)}, bf16[64,512]{1,0:T(8,128)(2,1)}) custom-call(bf16[128,1024]{1,0:T(8,128)(2,1)} %get-tuple-element.8.refs_0_, bf16[128,1024]{1,0:T(8,128)(2,1)} %get-tuple-element.9.refs_1_, bf16[64,768]{1,0:T(8,128)(2,1)} %get-tuple-element.10.refs_2_, ...), custom_call_target="tpu_custom_call" | custom-call | tf_op jit(solution)/shard_map/pallas_call | solution.py:709

commit v5 on v4

--- a/solution.py
+++ b/solution.py
@@ -119,33 +119,47 @@
     arrived(view(across, 1))
 
 
-def gather_columns(links, source, chosen, full):
+def gather_columns(links, source, chosen, full, first=0, count=None, x_first=False):
     y, x, z = links.y, links.x, links.z
-    place = full.at[y, x, z]
+    rows = pl.ds(first, count or source.shape[0])
+    place = full.at[y, x, z, rows]
     copies = [
-        links.copy(source.at[:, column(chosen(lax.rem(y + k, SIDE)))], place, links.along_y(k))
+        links.copy(
+            source.at[rows, column(chosen(lax.rem(y + k, SIDE)))], place, links.along_y(k)
+        )
         for k in (2, 1, 3)
     ]
     yield
     for made in copies:
         made.wait_recv()
-    block = full.at[:, x, z]
+    if x_first:
+        yield from ring_gather(
+            links,
+            links.along_x,
+            x,
+            lambda i, h: full.at[:, i, z] if h is None else full.at[pl.ds(2 * h, 2), i, z],
+        )
+        block = full.at[:, :, z]
+    else:
+        block = full.at[:, x, z, rows]
     copies = [links.copy(block, block, links.along_z(k)) for k in (2, 1, 3)]
     yield
     for made in copies:
         made.wait_recv()
-    yield from ring_gather(
-        links,
-        links.along_x,
-        x,
-        lambda i, h: full.at[:, i] if h is None else full.at[pl.ds(2 * h, 2), i],
-    )
-
-
-def gather_tokens(links, full):
+    if not x_first:
+        yield from ring_gather(
+            links,
+            links.along_x,
+            x,
+            lambda i, h: full.at[:, i, :, rows]
+            if h is None
+            else full.at[pl.ds(2 * h, 2), i, :, rows],
+        )
+
+
+def gather_tokens(links, full, handed):
     half = full.shape[1] // 2
     first = pl.multiple_of(links.core * half, half)
-    handed = []
 
     def view(i, h):
         if h is None:
@@ -157,7 +171,7 @@
 
     yield from ring_gather(links, links.along_y, links.y, view, hand)
     yield
-    for made in handed:
+    for made in handed[2:]:
         made.wait_recv()
 
 
@@ -435,13 +449,12 @@
     passed.wait_recv()
 
 
-def project(tokens, weight, target):
+def project(sequences, weight, target):
     size = 1024
 
     def step(i, carry):
-        rows = tokens[:, :, column(i, size)]
         part = jnp.dot(
-            rows.reshape(-1, size),
+            jnp.concatenate([tokens[:, column(i, size)] for tokens in sequences]),
             weight[i].reshape(size, HD),
             preferred_element_type=jnp.float32,
         ).reshape(target.shape)
@@ -451,42 +464,60 @@
     lax.fori_loop(0, SIDE, step, 0)
 
 
-def attend(query_pos, key_pos, cosine, sines, queries, head_grads, kv, heads_out, query_grad, totals):
-    score_scale = HD ** (-0.5)
+def attend(query_pos, key_pos, queries, kv, heads_out, raws, row_sums):
+    to_power = HD ** (-0.5) * float(np.log2(np.e))
     length = key_pos.shape[0]
     pair = 2
     rows = pair * queries.shape[1]
-    keys, values = kv[0].reshape(length, HD), kv[1].reshape(length, HD)
-    keys_t, values_t = keys.T, values.T
-    turn = jnp.concatenate([cosine[...]] * pair), jnp.concatenate([sines[...]] * pair)
-    totals[...] = jnp.zeros_like(totals)
+    keys = kv[0].reshape(length, HD)
+    values_t = kv[1].reshape(length, HD).T
 
     def step(i, carry):
         at = pl.ds(i * pair, pair)
-        q, grads = queries[at].reshape(rows, HD), head_grads[at].reshape(rows, HD)
+        q = queries[at].reshape(rows, HD)
         allowed = key_pos[...] <= query_pos[...]
-        scores = (
-            lax.dot_general(keys, q, contract_last, preferred_element_type=jnp.float32) * score_scale
-        )
+        scores = lax.dot_general(keys, q, contract_last, preferred_element_type=jnp.float32)
         scores = jnp.where(allowed, scores, masked_score)
         row_max = jnp.max(scores, axis=0, keepdims=True)
-        raw = jnp.where(allowed, jnp.exp(scores - row_max), 0.0)
+        raw = jnp.exp2((scores - row_max) * to_power)
+        raws[i] = raw
         row_sum = jnp.sum(raw, axis=0, keepdims=True)
+        row_sums[i] = row_sum
         weighted = jnp.dot(values_t, raw.astype(jnp.bfloat16), preferred_element_type=jnp.float32)
-        out = (weighted / row_sum).astype(jnp.bfloat16).astype(jnp.float32)
-        row_dots = jnp.sum(grads.astype(jnp.float32).T * out, axis=0, keepdims=True)
-        weights = raw * (1.0 / row_sum)
-        dweights = lax.dot_general(values, grads, contract_last, preferred_element_type=jnp.float32)
-        dscores = (weights * (dweights - row_dots)).astype(jnp.bfloat16)
-        heads_out[at] = out.T.astype(jnp.bfloat16).reshape(pair, -1, HD)
-        dq = jnp.dot(keys_t, dscores, preferred_element_type=jnp.float32).T * score_scale
-        dq = dq * turn[0] - pltpu.roll(dq, HD // 2, 1) * turn[1]
-        query_grad[at] = dq.astype(jnp.bfloat16).reshape(pair, -1, HD)
-        totals[0] += jnp.dot(dscores, q, preferred_element_type=jnp.float32) * score_scale
-        totals[1] += jnp.dot(weights.astype(jnp.bfloat16), grads, preferred_element_type=jnp.float32)
+        heads_out[at] = (weighted / row_sum).T.astype(jnp.bfloat16).reshape(pair, -1, HD)
         return carry
 
     lax.fori_loop(0, queries.shape[0] // pair, step, 0)
+
+
+def attend_back(
+    i, cosine, sines, queries, head_grads, kv, heads_out, raws, row_sums, query_grad, totals
+):
+    score_scale = HD ** (-0.5)
+    length = raws.shape[1]
+    pair = 2
+    rows = pair * queries.shape[1]
+    keys_t = kv[0].reshape(length, HD).T
+    values = kv[1].reshape(length, HD)
+    turn = jnp.concatenate([cosine[...]] * pair), jnp.concatenate([sines[...]] * pair)
+    at = pl.ds(i * pair, pair)
+    q, grads = queries[at].reshape(rows, HD), head_grads[at].reshape(rows, HD)
+    out = heads_out[at].reshape(rows, HD)
+    row_dots = jnp.sum(
+        (grads.astype(jnp.float32) * out.astype(jnp.float32)).T, axis=0, keepdims=True
+    )
+    weights = raws[i] * (1.0 / row_sums[i])
+    dweights = lax.dot_general(values, grads, contract_last, preferred_element_type=jnp.float32)
+    dscores = (weights * (dweights - row_dots)).astype(jnp.bfloat16)
+    dq = jnp.dot(keys_t, dscores, preferred_element_type=jnp.float32).T * score_scale
+    dq = dq * turn[0] - pltpu.roll(dq, HD // 2, 1) * turn[1]
+    query_grad[at] = dq.astype(jnp.bfloat16).reshape(pair, -1, HD)
+    key_part = jnp.dot(dscores, q, preferred_element_type=jnp.float32) * score_scale
+    value_part = jnp.dot(
+        weights.astype(jnp.bfloat16), grads, preferred_element_type=jnp.float32
+    )
+    totals[0] = key_part if i == 0 else totals[0] + key_part
+    totals[1] = value_part if i == 0 else totals[1] + value_part
 
 
 def place_tables(links, order, frequency, query_pos, key_pos, cosine, sines):
@@ -509,8 +540,8 @@
         key_pos[i * block : (i + 1) * block] = order[i] * block + row
 
 
-FRONT = "kqnokvqknoqdvkqnknoPdPVqKoQVdKVdoGKVvKV"
-BACK = "KVvbKVbaoKbmVoabKqVahonqmahwbqvewmnemqwnonowamnqw"
+FRONT = "joqknjdkjqknjkoqkoqjPvPVdvKonqvVKnQoVvdKdGKV"
+BACK = "ABBYXabaYsXfYaXrfbagvfYbXhgrubhwursgwfrsawgbsgrwswf"
 
 
 def whole_kernel(
@@ -526,7 +557,7 @@
     full_q, full_kv, full_out, full_other = weights
     my_queries, my_grads, queries, head_grads, heads_out, query_grad, all_heads = blocks
     projected, grads = wide
-    my_kv, all_kv, totals, kv_terms, handed = rows_kv
+    my_kv, all_kv, totals, kv_terms, handed, raws, row_sums = rows_kv
     after = lax.rem(y + 1, SIDE)
 
     given = {
@@ -546,19 +577,26 @@
     for k in (2, 3):
         grads[lax.rem(y + k, SIDE), :, HD:] = jnp.zeros_like(grads[0, :, HD:])
     links.greet()
-    streams = {name: gather_columns(links, *parts) for name, parts in given.items()}
-    streams["n"] = gather_tokens(links, all_normed)
-    streams["d"] = gather_tokens(links, all_d_out)
+    streams = {name: gather_columns(links, *given[name]) for name in "qo"}
+    half = w_qkv.shape[0] // 2
+    streams["k"] = gather_columns(links, *given["k"], 0, half)
+    streams["j"] = gather_columns(links, *given["k"], half, half)
+    streams["v"] = gather_columns(links, *given["v"], x_first=True)
+    handed_n, handed_d = [], []
+    streams["n"] = gather_tokens(links, all_normed, handed_n)
+    streams["d"] = gather_tokens(links, all_d_out, handed_d)
     for made in mine:
         made.wait()
-    in_order(streams, FRONT[:5])
+    in_order(streams, FRONT[:9])
     place_tables(links, order, frequency, query_pos, key_pos, cosine, sines)
     held = {}
 
     def project_kv():
-        for i, sequence in enumerate((y, after)):
-            project(all_normed.at[pl.ds(sequence, 1)], full_kv, projected.at[pl.ds(0, 1)])
-            part = projected[0]
+        for made in handed_n[:2]:
+            made.wait_recv()
+        project([all_normed.at[y], all_normed.at[after]], full_kv, projected.at[pl.ds(0, 2)])
+        for i in range(2):
+            part = projected[i]
             turned = part * cosine[...] + pltpu.roll(part, HD // 2, 1) * sines[...]
             my_kv[i] = jnp.where(lax.rem(y, 2) == 0, turned, part).astype(jnp.bfloat16)
         place = all_kv.at[lax.rem(y, 2), x, z]
@@ -568,7 +606,7 @@
         passed.wait_recv()
 
     def project_queries():
-        project(all_normed, full_q, projected)
+        project([all_normed.at[i] for i in range(SIDE)], full_q, projected)
         for i in range(SIDE):
             part = projected[i]
             turned = part * cosine[...] + pltpu.roll(part, HD // 2, 1) * sines[...]
@@ -577,7 +615,9 @@
         yield
 
     def project_grads():
-        project(all_d_out, full_out, projected)
+        for made in handed_d[:2]:
+            made.wait_recv()
+        project([all_d_out.at[i] for i in range(SIDE)], full_out, projected)
         my_grads[...] = projected[...].astype(jnp.bfloat16)
         held["G"] = exchange_heads(links, my_grads, head_grads.at[y], local.at[1])
         yield
@@ -587,14 +627,30 @@
     streams["G"] = project_grads()
     streams["K"] = gather_kind(links, all_kv.at[0])
     streams["V"] = gather_kind(links, all_kv.at[1])
-    in_order(streams, FRONT[5:])
-    arrive(held.pop("Q"))
-    arrive(held.pop("G"))
-    attend(query_pos, key_pos, cosine, sines, queries, head_grads, all_kv, heads_out, query_grad, totals)
-    kv_terms[...] = totals[...].astype(jnp.bfloat16).reshape(kv_terms.shape)
-
-    held["heads"] = exchange_heads(links, heads_out, all_heads.at[y], local.at[0])
-    held["grads"] = exchange_heads(links, query_grad, grads.at[y, :, pl.ds(0, HD)], local.at[1])
+
+    def attend_forward():
+        arrive(held.pop("Q"))
+        attend(query_pos, key_pos, queries, all_kv, heads_out, raws, row_sums)
+        held["heads"] = exchange_heads(links, heads_out, all_heads.at[y], local.at[0])
+        yield
+
+    def attend_backward():
+        arrive(held.pop("G"))
+        for i in range(2):
+            attend_back(
+                i, cosine, sines, queries, head_grads, all_kv, heads_out, raws, row_sums,
+                query_grad, totals,
+            )
+            if i == 0:
+                yield
+        kv_terms[...] = totals[...].astype(jnp.bfloat16).reshape(kv_terms.shape)
+        held["grads"] = exchange_heads(
+            links, query_grad, grads.at[y, :, pl.ds(0, HD)], local.at[1]
+        )
+        yield
+
+    streams["A"] = attend_forward()
+    streams["B"] = attend_backward()
 
     def having(name, stream):
         if name in held:
@@ -605,24 +661,21 @@
     own_terms, own_near = own
     query_part, kv_part = grads.at[:, :, pl.ds(0, HD)], grads.at[:, :, pl.ds(HD, HD)]
     own_pieces = [(grads.at[y, :, pl.ds(HD, HD)], full_kv), (handed, full_other)]
-    streams = {
-        "v": streams["v"],
-        "K": sum_kind(links, kv_terms.at[0], sums[0]),
-        "V": sum_kind(links, kv_terms.at[1], sums[1]),
-        "h": hand_kv(links, sums[0][3], sums[1][3], cosine, sines, grads, handed),
-        "e": own_groups(links, own_pieces, own_terms, own_near),
-        "w": sum_weight(links, all_normed, kv_part, sums[8]),
-    }
+    streams["X"] = sum_kind(links, kv_terms.at[0], sums[0])
+    streams["Y"] = sum_kind(links, kv_terms.at[1], sums[1])
+    streams["h"] = hand_kv(links, sums[0][3], sums[1][3], cosine, sines, grads, handed)
+    streams["u"] = own_groups(links, own_pieces, own_terms, own_near)
+    streams["w"] = sum_weight(links, all_normed, kv_part, sums[8])
     for name, needs, stream in (
         ("a", "heads", sum_groups(links, all_heads, full_out, attn_out, 0, sums[2])),
         ("b", "heads", sum_groups(links, all_heads, full_out, attn_out, half, sums[3])),
-        ("n", "grads", sum_groups(links, query_part, full_q, d_normed, 0, sums[4], own_terms)),
-        ("m", "grads", sum_groups(links, query_part, full_q, d_normed, half, sums[5], own_terms)),
-        ("o", "heads", sum_weight(links, all_d_out, all_heads, sums[6])),
-        ("q", "grads", sum_weight(links, all_normed, query_part, sums[7])),
+        ("r", "grads", sum_groups(links, query_part, full_q, d_normed, 0, sums[4], own_terms)),
+        ("s", "grads", sum_groups(links, query_part, full_q, d_normed, half, sums[5], own_terms)),
+        ("f", "heads", sum_weight(links, all_d_out, all_heads, sums[6])),
+        ("g", "grads", sum_weight(links, all_normed, query_part, sums[7])),
     ):
         streams[name] = having(needs, stream)
-    in_order(streams, BACK)
+    in_order(streams, FRONT[9:] + BACK)
     to_end(streams)
     links.finish()
     placed_out, placed_q, placed_kv = sums[6][5], sums[7][5], sums[8][5]
@@ -661,7 +714,7 @@
         return pltpu.VMEM(dims, kind)
 
     blocks = vmem(4, rows, HD)
-    copies = 4 * 10 + 2 * 8 + 1 + 2 * 7 + 4 * 3 + 2 * 9 + 1 + 2 + 4 * 9 + 3 * 12
+    copies = 5 * 10 + 2 * 8 + 1 + 2 * 7 + 4 * 3 + 2 * 9 + 1 + 2 + 4 * 9 + 3 * 12
     outs = [shape(rows, width), shape(rows, width), shape(*w_qkv.shape), shape(*w_out.shape)]
     results = pl.pallas_call(
         whole_kernel,
@@ -685,6 +738,8 @@
                 vmem(2, length, HD, kind=jnp.float32),
                 vmem(2, 4, 4, rows, HD),
                 vmem(rows, HD),
+                vmem(2, length, 2 * rows, kind=jnp.float32),
+                vmem(2, 1, 2 * rows, kind=jnp.float32),
             ),
             (vmem(4, rows, width), vmem(2, rows, width)),
             (sum_kind_scratch(rows),) * 2

time: 140 us -> 135 us (0.964); the launches traced: 140 us -> 133 us
  Pallas kernels: 140 us -> 132 us
    pallas_call x1, Pallas kernels: 138 us -> 130 us  [body(): pl.pallas_call(whole_kernel, out_shape=outs, in_specs=[HBM] * 4 + [pl.Blo...]
where the time goes in v5:
time: 135 us; the launch traced here: 133 us
  Pallas kernels  132 us (98%)
    pallas_call x1, Pallas kernels, body(): pl.pallas_call(whole_kernel, out_shape=outs, in_specs=[HBM] * 4 + [pl.Blo...  130 us

profile of v5, /device:TPU:64, one launch (start us, length us, event | category | flops | bytes accessed | tf_op | source)
XLA Modules:
  0.0 132.8 jit_solution(14912081698463801918)
XLA Ops:
  0.6 130.3 %shard_map.93 = (bf16[128,1024]{1,0:T(8,128)(2,1)}, bf16[128,1024]{1,0:T(8,128)(2,1)}, bf16[64,768]{1,0:T(8,128)(2,1)}, bf16[64,512]{1,0:T(8,128)(2,1)}) custom-call(bf16[1,128,4096]{2,1,0:T(8,128)(2,1)} %normed.1, bf16[1,128,4096]{2,1,0:T(8,128)(2,1)} %d_out.1, bf16[64,768]{1,0:T(8,128)(2,1)} %w_qkv.1, bf16[64,512]{1,0:T(8,128)(2,1)} %w_out.1, s32[32]{0:T(128)} %order.1, ...), custom_call_target="tpu_custom_call" | custom-call | tf_op jit(solution)/shard_map/pallas_call | solution.py:719
  130.9 1.9 %shard_map.94 = (bf16[1,128,1024]{2,1,0:T(8,128)(2,1)}, bf16[1,128,1024]{2,1,0:T(8,128)(2,1)}, bf16[64,768]{1,0:T(8,128)(2,1)}, bf16[64,512]{1,0:T(8,128)(2,1)}) custom-call(bf16[128,1024]{1,0:T(8,128)(2,1)} %get-tuple-element.8.refs_0_, bf16[128,1024]{1,0:T(8,128)(2,1)} %get-tuple-element.9.refs_1_, bf16[64,768]{1,0:T(8,128)(2,1)} %get-tuple-element.10.refs_2_, ...), custom_call_target="tpu_custom_call" | custom-call | tf_op jit(solution)/shard_map/pallas_call | solution.py:764

commit v6 on v5

--- a/solution.py
+++ b/solution.py
@@ -255,7 +255,7 @@
 
 
 def sum_weight(links, tokens, grads, scratch):
-    terms, ring, middle, arrived, summed, placed = scratch
+    terms, ring, middle, arrived, passed, summed, placed = scratch
     y, x, z = links.y, links.x, links.z
     size = 4 * terms.shape[3]
 
@@ -283,14 +283,20 @@
         ring,
         prepare,
     )
-    copies = [
-        links.copy(middle.at[:, lax.rem(z + k, SIDE)], arrived.at[k - 1], links.along_z(k))
-        for k in (2, 1, 3)
-    ]
-    yield
-    for made in copies:
-        made.wait_recv()
-    add_blocks(summed, middle.at[:, z], arrived.at[0], arrived.at[1], arrived.at[2])
+    step = 1 + 2 * lax.rem(z, 2)
+    neighbour, other = lax.rem(z + step, SIDE), lax.rem(z + 2, SIDE)
+    first = links.copy(
+        middle.at[:, lax.rem(neighbour + 2, SIDE)], arrived.at[0], links.along_z(step)
+    )
+    second = links.copy(middle.at[:, neighbour], arrived.at[1], links.along_z(step))
+    yield
+    first.wait_recv()
+    add_blocks(passed, middle.at[:, other], arrived.at[0])
+    third = links.copy(passed, arrived.at[2], links.along_z(2))
+    yield
+    second.wait_recv()
+    third.wait_recv()
+    add_blocks(summed, middle.at[:, z], arrived.at[1], arrived.at[2])
     copies = [
         links.copy(summed.at[lax.rem(y + k, SIDE)], placed.at[y], links.along_y(k))
         for k in (2, 1, 3)
@@ -306,7 +312,7 @@
         return pltpu.VMEM(dims + (rows, HD), jnp.bfloat16)
 
     ring = (vmem(2, 2, 4), vmem(2, 2, 4), vmem(2, 2, 4))
-    return (vmem(4, 4, 4), ring, vmem(4, 4), vmem(3, 4), vmem(4), vmem(4))
+    return (vmem(4, 4, 4), ring, vmem(4, 4), vmem(3, 4), vmem(4), vmem(4), vmem(4))
 
 
 def sum_groups(links, rows, weight, result, start, scratch, own_part=None):
@@ -540,8 +546,8 @@
         key_pos[i * block : (i + 1) * block] = order[i] * block + row
 
 
-FRONT = "joqknjdkjqknjkoqkoqjPvPVdvKonqvVKnQoVvdKdGKV"
-BACK = "ABBYXabaYsXfYaXrfbagvfYbXhgrubhwursgwfrsawgbsgrwswf"
+FRONT = "kqojnkdjokjjkqonjkPqovdqPKvVnKqVvnQdKVovdGKV"
+BACK = "ABBXYbabXYgbYXagrbvfaYXhgrfuahwsfrwugsafwgrsbwsrwgfsfw"
 
 
 def whole_kernel(
@@ -678,7 +684,7 @@
     in_order(streams, FRONT[9:] + BACK)
     to_end(streams)
     links.finish()
-    placed_out, placed_q, placed_kv = sums[6][5], sums[7][5], sums[8][5]
+    placed_out, placed_q, placed_kv = sums[6][6], sums[7][6], sums[8][6]
     width = SIDE * HD
     for j in range(SIDE):
         d_w_out[:, j * HD : (j + 1) * HD] = placed_out[j]

time: 135 us -> 133 us (0.985); the launches traced: 133 us -> 133 us
  no operation moved by 1% of the time
where the time goes in v6:
time: 133 us
  Pallas kernels  132 us (99%)
    pallas_call x1, Pallas kernels, body(): pl.pallas_call(whole_kernel, out_shape=outs, in_specs=[HBM] * 4 + [pl.Blo...  130 us

profile of v6, /device:TPU:64, one launch (start us, length us, event | category | flops | bytes accessed | tf_op | source)
XLA Modules:
  0.0 132.6 jit_solution(918087088587270935)
XLA Ops:
  0.6 130.0 %shard_map.93 = (bf16[128,1024]{1,0:T(8,128)(2,1)}, bf16[128,1024]{1,0:T(8,128)(2,1)}, bf16[64,768]{1,0:T(8,128)(2,1)}, bf16[64,512]{1,0:T(8,128)(2,1)}) custom-call(bf16[1,128,4096]{2,1,0:T(8,128)(2,1)} %normed.1, bf16[1,128,4096]{2,1,0:T(8,128)(2,1)} %d_out.1, bf16[64,768]{1,0:T(8,128)(2,1)} %w_qkv.1, bf16[64,512]{1,0:T(8,128)(2,1)} %w_out.1, s32[32]{0:T(128)} %order.1, ...), custom_call_target="tpu_custom_call" | custom-call | tf_op jit(solution)/shard_map/pallas_call | solution.py:725
  130.7 1.9 %shard_map.94 = (bf16[1,128,1024]{2,1,0:T(8,128)(2,1)}, bf16[1,128,1024]{2,1,0:T(8,128)(2,1)}, bf16[64,768]{1,0:T(8,128)(2,1)}, bf16[64,512]{1,0:T(8,128)(2,1)}) custom-call(bf16[128,1024]{1,0:T(8,128)(2,1)} %get-tuple-element.8.refs_0_, bf16[128,1024]{1,0:T(8,128)(2,1)} %get-tuple-element.9.refs_1_, bf16[64,768]{1,0:T(8,128)(2,1)} %get-tuple-element.10.refs_2_, ...), custom_call_target="tpu_custom_call" | custom-call | tf_op jit(solution)/shard_map/pallas_call | solution.py:770

commit v7 on v6

--- a/solution.py
+++ b/solution.py
@@ -221,7 +221,7 @@
     lax.fori_loop(0, count, step, 0)
 
 
-def ring_sum(links, along, here, view, result, scratch, prepare=None, extra=None):
+def ring_sum(links, along, here, view, result, scratch, prepare=None, extra=None, last=None):
     passing, from_left, from_right = scratch
     left, right, across = (
         lax.rem(here + 3, SIDE),
@@ -248,10 +248,18 @@
     yield
     plain_left.wait_recv()
     summed_right.wait_recv()
-    add_blocks(result(0), view(here, 0), from_left.at[0], from_right.at[0], *extra(0))
+
+    def parts(h):
+        return (view(here, h), from_left.at[h], from_right.at[h]) + tuple(extra(h))
+
+    if last is None:
+        add_blocks(result(0), *parts(0))
     plain_right.wait_recv()
     summed_left.wait_recv()
-    add_blocks(result(1), view(here, 1), from_left.at[1], from_right.at[1], *extra(1))
+    if last is None:
+        add_blocks(result(1), *parts(1))
+    else:
+        last(parts)
 
 
 def sum_weight(links, tokens, grads, scratch):
@@ -347,28 +355,35 @@
     for i in range(2):
         handed[i].wait_recv()
         add_blocks(terms.at[2 * i + core], terms.at[2 * i + core], near.at[i])
+    sums = []
+
+    def last(parts):
+        add_blocks(paired, *parts(1 - side))
+        sums.append(parts)
+
     yield from ring_sum(
         links,
         links.along_y,
         links.y,
         lambda i, h: terms.at[2 * h + core, i],
-        lambda h: paired.at[h],
+        None,
         ring,
+        last=last,
         extra=None
         if own_part is None
         else lambda h: (own_part.at[2 * h + core, :, pl.ds(start, width)],),
     )
-    across = links.copy(paired.at[1 - side], far, links.other_side())
+    across = links.copy(paired, far, links.other_side())
     yield
     across.wait_recv()
-    add_blocks(result.at[:, pl.ds(start, width)], paired.at[side], far)
+    add_blocks(result.at[:, pl.ds(start, width)], *sums[0](side), far)
 
 
 def sum_groups_scratch(rows, width):
     def vmem(*dims):
         return pltpu.VMEM(dims + (rows, width), jnp.bfloat16)
 
-    return (vmem(4, 4), vmem(2, 4), (vmem(2), vmem(2), vmem(2)), vmem(2), vmem())
+    return (vmem(4, 4), vmem(2, 4), (vmem(2), vmem(2), vmem(2)), vmem(), vmem())
 
 
 def model_rows(weight, i, size):

time: 133 us -> 133 us (level)
  no operation moved by 1% of the time
where the time goes in v7:
time: 133 us
  Pallas kernels  132 us (99%)
    pallas_call x1, Pallas kernels, body(): pl.pallas_call(whole_kernel, out_shape=outs, in_specs=[HBM] * 4 + [pl.Blo...  130 us

profile of v7, /device:TPU:64, one launch (start us, length us, event | category | flops | bytes accessed | tf_op | source)
XLA Modules:
  0.0 132.5 jit_solution(17283336020099616375)
XLA Ops:
  0.6 130.0 %shard_map.93 = (bf16[128,1024]{1,0:T(8,128)(2,1)}, bf16[128,1024]{1,0:T(8,128)(2,1)}, bf16[64,768]{1,0:T(8,128)(2,1)}, bf16[64,512]{1,0:T(8,128)(2,1)}) custom-call(bf16[1,128,4096]{2,1,0:T(8,128)(2,1)} %normed.1, bf16[1,128,4096]{2,1,0:T(8,128)(2,1)} %d_out.1, bf16[64,768]{1,0:T(8,128)(2,1)} %w_qkv.1, bf16[64,512]{1,0:T(8,128)(2,1)} %w_out.1, s32[32]{0:T(128)} %order.1, ...), custom_call_target="tpu_custom_call" | custom-call | tf_op jit(solution)/shard_map/pallas_call | solution.py:740
  130.6 1.9 %shard_map.94 = (bf16[1,128,1024]{2,1,0:T(8,128)(2,1)}, bf16[1,128,1024]{2,1,0:T(8,128)(2,1)}, bf16[64,768]{1,0:T(8,128)(2,1)}, bf16[64,512]{1,0:T(8,128)(2,1)}) custom-call(bf16[128,1024]{1,0:T(8,128)(2,1)} %get-tuple-element.8.refs_0_, bf16[128,1024]{1,0:T(8,128)(2,1)} %get-tuple-element.9.refs_1_, bf16[64,768]{1,0:T(8,128)(2,1)} %get-tuple-element.10.refs_2_, ...), custom_call_target="tpu_custom_call" | custom-call | tf_op jit(solution)/shard_map/pallas_call | solution.py:785
